TPU v7x, 32 devices: a whole 2x2x4 slice. The times are simulated.
32 devices in a mesh: tok: 4 (over x, core), head: 8 (over z, y).
Axes of the slice: x: 2, y: 2, z: 4, core: 2. Of those that a mesh axis runs over, the one named last changes fastest.
Arguments:
- q_nope: bfloat16 [512, 16384], P('tok', 'head'), may hold values from -6 to 6
- q_rope: bfloat16 [512, 8192], P('tok', 'head'), may hold values from -10 to 10
- cache_kv: bfloat16 [512, 576], P('tok'), may hold values from -6 to 6
- span_kv: bfloat16 [512, 576], P('tok'), may hold values from -6 to 6
- w_uk: bfloat16 [512, 16384], P(None, 'head'), may hold values from -0.5 to 0.5
- w_uv: bfloat16 [512, 16384], P(None, 'head'), may hold values from -3 to 3
- w_o: bfloat16 [16384, 7168], P('head', 'tok'), may hold values from -0.046875 to 0.046875
- prefix_length: int32 [1], replicated, may hold values from 256 to 512
Outputs:
- attn_out: bfloat16 [512, 7168], P('head', 'tok')
All inputs are finite; a program needn't handle non-finite values.
Results may differ from a plain program's by a relative error of at most 0.014.
Values may be sent and summed in bfloat16 or wider, within the bound.
No kernel may reach another device: no remote copies, remote signals or barrier semaphores. Data moves between devices by JAX's collectives and lax.ppermute only.
A program may use at most 64 MiB of HBM per device.

v0:
```python
import math

import jax
import jax.numpy as jnp
from jax import lax
from jax.sharding import PartitionSpec as P

DN = 128
DR = 64
DV = 128
KVL = 512


MASKED = -1e30


def shards(q_nope, q_rope, cache_kv, span_kv, w_uk, w_uv, w_o, prefix_length):
    tok_rows = q_nope.shape[0]
    head_count = w_uk.shape[1] // DN
    cache_rows = cache_kv.shape[0]
    key_block = cache_rows + tok_rows
    query_rows = tok_rows * head_count
    score_scale = 1.0 / math.sqrt(DN + DR)
    query_latent = (
        jnp.einsum(
            "thn,khn->thk",
            q_nope.reshape(tok_rows, head_count, DN),
            w_uk.reshape(KVL, head_count, DN),
            preferred_element_type=jnp.float32,
        )
        .astype(jnp.bfloat16)
        .reshape(query_rows, KVL)
    )
    query_rotary = q_rope.reshape(query_rows, DR)
    query_token = (
        lax.axis_index("tok") * tok_rows + jnp.arange(query_rows, dtype=jnp.int32) // head_count
    )
    live_limit = prefix_length[0]
    contract = (((1,), (1,)), ((), ()))
    local_keys = jnp.concatenate([cache_kv, span_kv], 0)
    key_piece = lax.all_gather(local_keys, "tok", axis=0, tiled=True)
    key_index = jnp.arange(key_piece.shape[0], dtype=jnp.int32)
    key_owner = key_index // key_block
    key_offset = key_index % key_block
    top_score = jnp.full((query_rows,), MASKED, jnp.float32)
    is_cached = key_offset < cache_rows
    live_cache = key_owner * cache_rows + key_offset < live_limit
    live_span = (key_owner * tok_rows + key_offset - cache_rows)[None, :] <= query_token[:, None]
    is_live = jnp.where(is_cached[None, :], live_cache[None, :], live_span)
    key_latent = key_piece[:, :KVL]
    key_rotary = key_piece[:, KVL:]
    scores = lax.dot_general(query_latent, key_latent, contract, preferred_element_type=jnp.float32)
    scores = scores + lax.dot_general(
        query_rotary, key_rotary, contract, preferred_element_type=jnp.float32
    )
    scores = jnp.where(is_live, scores * score_scale, MASKED)
    new_top = jnp.maximum(top_score, jnp.max(scores, axis=1))
    weights = jnp.where(is_live, jnp.exp(scores - new_top[:, None]), 0.0)
    weight_sum = jnp.sum(weights, axis=1)
    value_sum = jnp.dot(
        weights.astype(jnp.bfloat16), key_latent, preferred_element_type=jnp.float32
    )
    top_score, weight_sum, value_sum = (new_top, weight_sum, value_sum)
    latent_out = (
        (value_sum / weight_sum[:, None]).astype(jnp.bfloat16).reshape(tok_rows, head_count, KVL)
    )
    value_out = (
        jnp.einsum(
            "thk,khv->thv",
            latent_out,
            w_uv.reshape(KVL, head_count, DV),
            preferred_element_type=jnp.float32,
        )
        .astype(jnp.bfloat16)
        .reshape(tok_rows, head_count * DV)
    )
    partial_rows = jnp.dot(
        lax.all_gather(value_out, "tok", axis=0, tiled=True),
        w_o,
        preferred_element_type=jnp.float32,
    )
    summed = lax.psum_scatter(
        partial_rows.astype(jnp.bfloat16), "head", scatter_dimension=0, tiled=True
    )
    return summed


def solution(mesh):
    return jax.shard_map(
        shards,
        mesh=mesh,
        in_specs=(
            P("tok", "head"),
            P("tok", "head"),
            P("tok", None),
            P("tok", None),
            P(None, "head"),
            P(None, "head"),
            P("head", "tok"),
            P(),
        ),
        out_specs=P("head", "tok"),
        check_vma=False,
    )
```

profile of v0, /device:TPU:0, one launch (start us, length us, event | category | flops | bytes accessed | tf_op | source)
XLA Modules:
  0.0 151.5 jit_solution(13510713361288151194)
XLA Ops:
  6.5 0.0 copy-start
  6.5 0.0 all-gather.3.cloned.1.call-start
  6.5 1.9 %pad_maximum_fusion = bf16[256,576]{0,1:T(8,128)(2,1)} fusion(bf16[128,576]{0,1:T(8,128)(2,1)} %param.11, bf16[128,576]{0,1:T(8,128)(2,1)} %param.10), kind=kLoop, calls=%fused_computation.28 | loop fusion | flops 589824 | bytes 589824 | tf_op jit(solution)/shard_map/concatenate | solution.py:40
  8.4 0.0 all-gather.3.cloned.1.call-update
  8.5 0.0 all-gather.5.cloned.1.call-start
  9.2 0.0 copy-done
  9.2 1.8 %convert_bitcast_fusion = bf16[128,16,512]{2,0,1:T(8,128)(2,1)S(1)} fusion(bf16[512,2048]{1,0:T(8,128)(2,1)S(1)} %copy-done, bf16[128,2048]{1,0:T(8,128)(2,1)} %param.8), kind=kOutput, calls=%fused_computation.21 | convolution fusion | flops 269484032 | bytes 4718592 | tf_op jit(solution)/shard_map/thn,khn->thk/dot_general | solution.py:25
  10.9 0.0 copy-start.2
  10.9 2.5 %copy.15 = bf16[128,16,512]{2,1,0:T(8,128)(2,1)} copy(bf16[128,16,512]{2,0,1:T(8,128)(2,1)S(1)} %convert_bitcast_fusion) | data formatting | bytes 4194304 | tf_op jit(solution)/shard_map/convert_element_type | solution.py:31
  13.4 0.3 reshape.73
  13.8 3.9 %copy.18 = bf16[512,2048]{0,1:T(8,128)(2,1)} copy(bf16[512,2048]{1,0:T(8,128)(2,1)} %param.13) | data formatting | bytes 4194304 | tf_op jit(solution)/shard_map/reshape | solution.py:71
  17.7 11.5 %all-gather.3.cloned.1.call-done = bf16[1024,576]{0,1:T(8,128)(2,1)} async-done(((bf16[256,576]{0,1:T(8,128)(2,1)}), bf16[1024,576]{0,1:T(8,128)(2,1)}) %all-gather.3.cloned.1.call-update) | async-done | bytes 1179664 | tf_op jit(solution)/shard_map/all_gather | solution.py:41
  29.2 4.4 %fusion.25 = f32[2048,1024]{0,1:T(8,128)S(1)} fusion(bf16[2048,512]{1,0:T(8,128)(2,1)} %bitcast.38, bf16[1024,576]{0,1:T(8,128)(2,1)} %all-gather.3.cloned.1.call-done), kind=kOutput, calls=%fused_computation.24 | convolution fusion | flops 2147483648 | bytes 11534336 | tf_op jit(solution)/shard_map/dot_general | solution.py:52
  33.6 3.3 %fusion.45 = (f32[2048]{0:T(1024)S(1)}, f32[2048,1024]{0,1:T(8,128)S(1)}) fusion(f32[2048,1024]{0,1:T(8,128)S(1)} %fusion.25, bf16[2048,64]{1,0:T(8,128)(2,1)S(1)} %reshape.73, bf16[1024,576]{0,1:T(8,128)(2,1)S(1)} %copy-done.3, s32[2048]{0:T(1024)S(1)} %fusion.30, s32[1024]{0:T(1024)S(1)} %fusion.42, pred[1024]{0:T(1024)(128)(4,1)S(1)} %get-tuple-element.8, ...), kind=kOutput, calls=%fused_computation.55 | convolution fusion | flops 281016320 | bytes 17455104 | tf_op jit(solution)/shard_map/dot_general | solution.py:53
  37.0 3.3 %fusion.2 = f32[2048]{0:T(1024)S(1)} fusion(f32[2048,1024]{0,1:T(8,128)S(1)} %get-tuple-element.6, f32[2048]{0:T(1024)S(1)} %broadcast_maximum_fusion, s32[2048]{0:T(1024)S(1)} %fusion.30, s32[1024]{0:T(1024)S(1)} %fusion.42, pred[1024]{0:T(1024)(128)(4,1)S(1)} %get-tuple-element.8, pred[1024]{0:T(1024)(128)(4,1)S(1)} %get-tuple-element.7), kind=kLoop, calls=%fused_computation.5 | loop fusion | flops 10483712 | bytes 8419328 | tf_op jit(solution)/shard_map/reduce_sum | solution.py:59
  40.3 3.8 %divide_convert_fusion = bf16[2048,512]{1,0:T(8,128)(2,1)S(1)} fusion(f32[2048]{0:T(1024)S(1)} %fusion.2, f32[2048,1024]{0,1:T(8,128)S(1)} %get-tuple-element.6, f32[2048]{0:T(1024)S(1)} %broadcast_maximum_fusion, s32[2048]{0:T(1024)S(1)} %fusion.30, s32[1024]{0:T(1024)S(1)} %fusion.42, pred[1024]{0:T(1024)(128)(4,1)S(1)} %get-tuple-element.8, ...), kind=kOutput, calls=%fused_computation.8 | convolution fusion | flops 2160066560 | bytes 11565056 | tf_op jit(solution)/shard_map/dot_general | solution.py:60
  44.1 0.0 copy-done.1
  44.1 2.3 %fusion.21 = bf16[16,128,128]{1,2,0:T(8,128)(2,1)} fusion(bf16[512,16,128]{0,2,1:T(8,128)(2,1)S(1)} %bitcast.37, bf16[128,16,512]{2,1,0:T(8,128)(2,1)S(1)} %bitcast.40), kind=kOutput, calls=%fused_computation.22 | convolution fusion | flops 268697600 | bytes 4718592 | tf_op jit(solution)/shard_map/thk,khv->thv/dot_general | solution.py:68
  46.4 0.0 all-gather.5.cloned.1.call-update
  46.4 0.0 reduce-scatter.2.cloned.1.call-start
  46.5 22.9 %all-gather.5.cloned.1.call-done = bf16[512,2048]{0,1:T(8,128)(2,1)} async-done(((bf16[128,2048]{0,1:T(8,128)(2,1)}), bf16[512,2048]{0,1:T(8,128)(2,1)}) %all-gather.5.cloned.1.call-update) | async-done | bytes 2097168 | tf_op jit(solution)/shard_map/all_gather | solution.py:78
  69.4 9.0 %convolution_convert_fusion = bf16[512,1792]{1,0:T(8,128)(2,1)} fusion(bf16[512,2048]{0,1:T(8,128)(2,1)} %all-gather.5.cloned.1.call-done, bf16[2048,1792]{1,0:T(8,128)(2,1)} %param.14), kind=kOutput, calls=%fused_computation.15 | convolution fusion | flops 3759013888 | bytes 11272192 | tf_op jit(solution)/shard_map/dot_general | solution.py:77
  78.4 0.0 reduce-scatter.2.cloned.1.call-update
  78.5 66.5 %reduce-scatter.2.cloned.1.call-done = bf16[64,1792]{1,0:T(8,128)(2,1)} async-done(((bf16[512,1792]{1,0:T(8,128)(2,1)}), bf16[64,1792]{1,0:T(8,128)(2,1)}) %reduce-scatter.2.cloned.1.call-update) | async-done | bytes 229392 | tf_op jit(solution)/shard_map/reduce_scatter | solution.py:82
  (8 shorter events, 0.0 us)
Async XLA Ops:
  6.5 2.6 %copy-start = (bf16[512,2048]{1,0:T(8,128)(2,1)S(1)}, bf16[512,2048]{1,0:T(8,128)(2,1)}, u32[]{:S(2)}) copy-start(bf16[512,2048]{1,0:T(8,128)(2,1)} %param.12) | copy-start | bytes 6291460
  6.5 22.7 %all-gather.3.cloned.1.call-start = ((), (), s32[]{:S(2)}) async-start(), calls=%async_computation.1 | async-start | bytes 1474560 | tf_op jit(solution)/shard_map/all_gather | solution.py:41
  8.5 61.0 %all-gather.5.cloned.1.call-start = ((), (), s32[]{:S(2)}) async-start(), calls=%async_computation.2 | async-start | bytes 2621440 | tf_op jit(solution)/shard_map/all_gather | solution.py:78
  10.9 2.5 %copy-start.2 = (bf16[128,1024]{1,0:T(8,128)(2,1)S(1)}, bf16[128,1024]{1,0:T(8,128)(2,1)}, u32[]{:S(2)}) copy-start(bf16[128,1024]{1,0:T(8,128)(2,1)} %param.9) | copy-start | bytes 786436
  29.2 4.4 %copy-start.3 = (bf16[1024,576]{0,1:T(8,128)(2,1)S(1)}, bf16[1024,576]{0,1:T(8,128)(2,1)}, u32[]{:S(2)}) copy-start(bf16[1024,576]{0,1:T(8,128)(2,1)} %all-gather.3.cloned.1.call-done) | copy-start | bytes 3538948
  40.3 3.8 %copy-start.1 = (bf16[512,2048]{0,1:T(8,128)(2,1)S(1)}, bf16[512,2048]{0,1:T(8,128)(2,1)}, u32[]{:S(2)}) copy-start(bf16[512,2048]{0,1:T(8,128)(2,1)} %copy.18) | copy-start | bytes 6291460
  46.4 98.5 %reduce-scatter.2.cloned.1.call-start = ((), (), s32[]{:S(2)}) async-start(), calls=%async_computation.3 | async-start | bytes 2064384 | tf_op jit(solution)/shard_map/reduce_scatter | solution.py:82
Sparse Core Ops, SparseCore 0:
  8.9 20.2 all-gather.2
  46.6 22.8 all-gather.4
  78.6 66.3 reduce-scatter.1
where the time goes:
time: 152 us
  waiting for transfers between devices  101 us (66%)
  matrix products  24.6 us (16%)
  between operations  13.9 us (9%)
  local copies, waits for them, and re-layouts  6.77 us (4%)
  other arithmetic  5.22 us (3%)
    reduce_scatter x1, waiting for transfers between devices, shards(): lax.psum_scatter(partial_rows.astype(jnp.bfloat16), 'head', scatter_dimen...  66.5 us
    all_gather x1, waiting for transfers between devices, shards(): lax.all_gather(value_out, 'tok', axis=0, tiled=True)  22.9 us
    all_gather x1, waiting for transfers between devices, shards(): key_piece = lax.all_gather(local_keys, 'tok', axis=0, tiled=True)  11.5 us
    dot_general x1, matrix products, shards(): jnp.dot(lax.all_gather(value_out, 'tok', axis=0, tiled=True), w_o, prefer...  8.98 us
    dot_general x1, matrix products, shards(): lax.dot_general(query_latent, key_latent, contract, preferred_element_typ...  4.38 us
    reshape x1, local copies, waits for them, and re-layouts, shards(): w_uv.reshape(KVL, head_count, DV)  3.93 us
    dot_general x1, matrix products, shards(): jnp.dot(weights.astype(jnp.bfloat16), key_latent, preferred_element_type=...  3.81 us
    dot_general x1, matrix products, shards(): lax.dot_general(query_rotary, key_rotary, contract, preferred_element_typ...  3.32 us
  transfers between devices with their start and end apart: 3, of which 3 were waited for; matrix products, arithmetic and copies ran while one was open for 6% of the time, Pallas kernels for 0%

commit v1 on v0

v1 whole, which is shorter than its diff:
```python
import functools
import math

import jax
import jax.numpy as jnp
from jax import lax
from jax.experimental import pallas as pl
from jax.experimental.pallas import tpu as pltpu
from jax.sharding import PartitionSpec as P

DN = 128
DR = 64
DV = 128
KVL = 512
KD = KVL + DR

MASKED = -1e30
CHUNKS = 2
FIRST = 0.72
COST_SHARE = 1
VMEM_LIMIT = 24 * 1024 * 1024
EXP_SCALE = math.log2(math.e) / math.sqrt(DN + DR)

f32 = jnp.float32
bf16 = jnp.bfloat16


def dot(a, b):
    return jnp.dot(a, b, preferred_element_type=f32)


def dot_t(a, b):
    return lax.dot_general(a, b, (((1,), (1,)), ((), ())), preferred_element_type=f32)


def xor_permute(x, axis, bit):
    n = lax.axis_size(axis)
    return lax.ppermute(x, axis, [(i, i ^ bit) for i in range(n)])


def bits_of(n):
    return [1 << i for i in range(n.bit_length() - 1)]


def in_vmem(x):
    return pltpu.with_memory_space_constraint(x, pltpu.VMEM)


def load_keys(caches, spans, rels, limit, tokens, kt, k, bias):
    me = lax.axis_index("tok")
    rows = bias.shape[0]
    half = tokens // 2
    part = half // CHUNKS
    row = lax.broadcasted_iota(jnp.int32, (rows, 1), 0)
    chunk, rest = row // (rows // CHUNKS), row % (rows // CHUNKS)
    token = (rest // part) * half + chunk * part + rest % part
    cached = caches[0].shape[1]
    size = cached + tokens
    for at, (cache, span, rel) in enumerate(zip(caches, spans, rels)):
        owner = me ^ rel
        start = at * size
        kt[:, start : start + cached] = cache[...]
        kt[:, start + cached : start + size] = span[...]
        column = lax.broadcasted_iota(jnp.int32, (rows, cached), 1)
        bias[:, start : start + cached] = jnp.where(owner * cached + column < limit, 0.0, MASKED)
        column = lax.broadcasted_iota(jnp.int32, (rows, tokens), 1)
        bias[:, start + cached : start + size] = jnp.where(
            owner * tokens + column <= me * tokens + token, 0.0, MASKED
        )
    k[...] = kt[:KVL, :].T


def split_refs(refs, *counts):
    out, at = [], 0
    for count in counts:
        out.append(refs[at : at + count])
        at += count
    return out + [refs[at:]]


def query_kernel(tokens, group, qn, qr, wuk, q_out, nope, rotary, up, sems):
    half = tokens // 2
    part = half // CHUNKS
    rows = tokens // CHUNKS
    steps = q_out.shape[1] // group

    def copies(i):
        wide = pl.ds(pl.multiple_of(i * group * DN, group * DN), group * DN)
        narrow = pl.ds(pl.multiple_of(i * group * DR, group * DR), group * DR)
        return [
            pltpu.make_async_copy(src.at[:, at], dst.at[:, at], sems.at[i, j])
            for j, (src, dst, at) in enumerate(
                ((wuk, up, wide), (qn, nope, wide), (qr, rotary, narrow))
            )
        ]

    for i in range(steps):
        for copy in copies(i):
            copy.start()

    def ordered(x):
        return jnp.concatenate(
            [
                x[b * half + c * part : b * half + (c + 1) * part]
                for c in range(CHUNKS)
                for b in range(2)
            ],
            0,
        )

    def step(i, _):
        for copy in copies(i):
            copy.wait()
        wide = pl.ds(pl.multiple_of(i * group * DN, group * DN), group * DN)
        narrow = pl.ds(pl.multiple_of(i * group * DR, group * DR), group * DR)
        n, r, w = nope[:, wide], rotary[:, narrow], up[:, wide]
        for g in range(group):
            latent = dot_t(n[:, g * DN : (g + 1) * DN], w[:, g * DN : (g + 1) * DN])
            latent = ordered(latent.astype(bf16))
            rope = ordered(r[:, g * DR : (g + 1) * DR])
            for c in range(CHUNKS):
                q_out[c, i * group + g, :, :KVL] = latent[c * rows : (c + 1) * rows]
                q_out[c, i * group + g, :, KVL:] = rope[c * rows : (c + 1) * rows]
        return 0

    lax.fori_loop(0, steps, step, 0)


def local_kernel(rels, tokens, group, *refs):
    n = len(rels)
    (limit, q), caches, spans, (acc_out, ml_out), (kt, k, bias) = split_refs(refs, 2, n, n, 2)
    load_keys(caches, spans, rels, limit[0], tokens, kt, k, bias)
    rows = tokens // CHUNKS
    keys = kt.shape[1]
    steps = q.shape[1] // group

    def step(i, _):
        c = i // steps
        heads = pl.ds((i % steps) * group, group)
        s = dot(q[c, heads].reshape(group * rows, KD), kt[...]).reshape(group, rows, keys)
        s = s + bias[pl.ds(pl.multiple_of(c * rows, rows), rows)][None]
        m = jnp.max(s, axis=2, keepdims=True)
        p = jnp.exp2((s - m) * EXP_SCALE)
        l = jnp.sum(p, axis=2, keepdims=True)
        o = dot(p.astype(bf16).reshape(group * rows, keys), k[...])
        lane = lax.broadcasted_iota(jnp.int32, (group, rows, 128), 2)
        acc_out[c, heads] = o.reshape(group, rows, KVL)
        ml_out[c, heads] = jnp.where(lane < 64, m, l)
        return 0

    lax.fori_loop(0, CHUNKS * steps, step, 0)


def rest_kernel(rels, tokens, group, which, *refs):
    n = len(rels)
    (limit, q, acc, ml, wuv), caches, spans, (out,), (kt, k, bias) = split_refs(refs, 5, n, n, 1)
    rows = tokens // CHUNKS
    load_keys(caches, spans, rels, limit[0], tokens, kt, k, bias)
    keys = kt.shape[1]

    def step(i, _):
        heads = pl.ds(i * group, group)
        columns = pl.ds(pl.multiple_of(i * group * DV, group * DV), group * DV)
        s = dot(q[which, heads].reshape(group * rows, KD), kt[...]).reshape(group, rows, keys)
        s = s + bias[which * rows : (which + 1) * rows][None]
        both = ml[which, heads]
        m1 = both[:, :, :1]
        l1 = both[:, :, 64:65]
        m = jnp.maximum(m1, jnp.max(s, axis=2, keepdims=True))
        p = jnp.exp2((s - m) * EXP_SCALE)
        a = jnp.exp2((m1 - m) * EXP_SCALE)
        l = l1 * a + jnp.sum(p, axis=2, keepdims=True)
        o = dot(p.astype(bf16).reshape(group * rows, keys), k[...]).reshape(group, rows, KVL)
        o = ((acc[which, heads] * a + o) / l).astype(bf16)
        up = wuv[:, columns]
        out[:, columns] = jnp.concatenate(
            [dot(o[g], up[:, g * DV : (g + 1) * DV]).astype(bf16) for g in range(group)], 1
        )
        return 0

    lax.fori_loop(0, q.shape[1] // group, step, 0)


def first_last(bits):
    if not bits:
        return [0]
    rest = first_last(bits[1:])
    return [bits[0] | x for x in rest] + rest


def project_kernel(n_tok, per, groups, *refs):
    pieces, (w_o,), outs, (lhs,) = split_refs(refs, n_tok, 1, 2 * len(groups))
    part = pieces[0].shape[0] // per
    n = n_tok * per
    bits = groups[0][0]
    order = first_last(bits)
    me_tok, me_head = lax.axis_index("tok"), lax.axis_index("head")
    for i in range(n_tok):
        for b in range(per):
            rel = ((me_tok ^ i) * per + b) ^ me_head
            at = jnp.int32(0)
            for step, bit in enumerate(bits):
                at = at + jnp.where(rel & bit == 0, n >> (step + 1), 0)
            start = pl.multiple_of(at * part, part)
            lhs[pl.ds(start, part), :] = pieces[i][b * part : (b + 1) * part, :]
    rows = n * part // 2
    for j, (own, start, count, tile) in enumerate(groups):
        send, keep = outs[2 * j : 2 * j + 2]
        for t in range(count):
            columns = slice((start + t) * tile, (start + t + 1) * tile)
            here = slice(t * tile, (t + 1) * tile)
            y = dot(lhs[...], w_o[:, columns]).astype(bf16)
            if own != bits:
                y = jnp.concatenate(
                    [y[order.index(r) * part :][:part] for r in first_last(own)], 0
                )
            send[:, here] = y[:rows]
            keep[:, here] = y[rows:]


def shards(q_nope, q_rope, cache_kv, span_kv, w_uk, w_uv, w_o, prefix_length):
    tokens = q_nope.shape[0]
    heads = w_uk.shape[1] // DN
    cache_rows = cache_kv.shape[0]
    n_tok, n_head = lax.axis_size("tok"), lax.axis_size("head")
    per = n_head // n_tok
    rows = tokens // CHUNKS
    params = pltpu.CompilerParams(vmem_limit_bytes=VMEM_LIMIT)
    smem = pl.BlockSpec(memory_space=pltpu.SMEM)
    vmem = pl.BlockSpec(memory_space=pltpu.VMEM)

    def step(held, axis_bit):
        return {rel ^ axis_bit: xor_permute(v, "tok", axis_bit) for rel, v in held.items()}

    def gather(x):
        held = {0: x}
        for bit in reversed(bits_of(n_tok)):
            held.update(step(held, bit))
        return [in_vmem(held[rel]) for rel in range(n_tok)]

    def cost(flops):
        return pl.CostEstimate(flops=flops // COST_SHARE, bytes_accessed=0, transcendentals=0)

    held = {0: (cache_kv.T, span_kv.T)}

    def key_step(held, bit):
        return {
            rel ^ bit: tuple(xor_permute(v, "tok", bit) for v in both)
            for rel, both in held.items()
        }

    for bit in reversed(bits_of(n_tok)[1:]):
        held.update(key_step(held, bit))
    held.update(key_step({0: held[0]}, 1))
    caches = {rel: in_vmem(held[rel][0]) for rel in (0, 1)}
    spans = {rel: in_vmem(held[rel][1]) for rel in (0, 1)}
    near = [rel for rel in range(n_tok) if rel < 2]
    far = [rel for rel in range(n_tok) if rel >= 2]

    def key_scratch(rels):
        keys = len(rels) * (cache_rows + tokens)
        return [
            pltpu.VMEM((KD, keys), bf16),
            pltpu.VMEM((keys, KVL), bf16),
            pltpu.VMEM((tokens, keys), f32),
        ]

    group = math.gcd(heads, 4)
    anywhere = pl.BlockSpec(memory_space=pltpu.HBM)
    q = in_vmem(
        pl.pallas_call(
            functools.partial(query_kernel, tokens, group),
            in_specs=[anywhere] * 3,
            out_specs=vmem,
            out_shape=pltpu.VMEM((CHUNKS, heads, rows, KD), bf16),
            scratch_shapes=[
                pltpu.VMEM(q_nope.shape, bf16),
                pltpu.VMEM(q_rope.shape, bf16),
                pltpu.VMEM(w_uk.shape, bf16),
                pltpu.SemaphoreType.DMA((heads // group, 3)),
            ],
            compiler_params=params,
            name="query_latent",
            cost_estimate=cost(2 * tokens * w_uk.size),
        )(*[pltpu.with_memory_space_constraint(x, pltpu.HBM) for x in (q_nope, q_rope, w_uk)])
    )
    group = math.gcd(heads, 8)
    acc, ml = pl.pallas_call(
        functools.partial(local_kernel, near, tokens, group),
        in_specs=[smem] + [vmem] * (1 + 2 * len(near)),
        out_specs=[vmem] * 2,
        out_shape=[
            pltpu.VMEM((CHUNKS, heads, rows, KVL), f32),
            pltpu.VMEM((CHUNKS, heads, rows, 128), f32),
        ],
        scratch_shapes=key_scratch(near),
        compiler_params=params,
        name="local_keys",
        cost_estimate=cost(4 * tokens * heads * len(near) * (cache_rows + tokens) * KD),
    )(prefix_length, q, *[caches[r] for r in near], *[spans[r] for r in near])
    acc, ml = in_vmem(acc), in_vmem(ml)
    others = {rel: both for rel, both in held.items() if rel > 1}
    others, acc, ml = lax.optimization_barrier((others, acc, ml))
    others.update(key_step(others, 1))
    caches.update({rel: in_vmem(both[0]) for rel, both in others.items()})
    spans.update({rel: in_vmem(both[1]) for rel, both in others.items()})
    acc, ml = in_vmem(acc), in_vmem(ml)

    def rest(which):
        return pl.pallas_call(
            functools.partial(rest_kernel, far, tokens, group, which),
            in_specs=[smem] + [vmem] * (4 + 2 * len(far)),
            out_specs=vmem,
            out_shape=pltpu.VMEM((rows, heads * DV), bf16),
            scratch_shapes=key_scratch(far),
            compiler_params=params,
            name="far_keys",
            cost_estimate=cost(4 * rows * heads * len(far) * (cache_rows + tokens) * KD),
        )(prefix_length, q, acc, ml, in_vmem(w_uv), *[caches[r] for r in far], *[spans[r] for r in far])

    columns = w_o.shape[1]
    depth = w_o.shape[0]
    tile = 256 if columns % 256 == 0 else columns
    tiles = columns // tile
    low = bits_of(n_head)
    first = max(1, int(tiles * FIRST))
    groups = [(low, 0, first, tile)]
    if first < tiles:
        groups.append((low[1:] + low[:1], first, tiles - first, tile))

    def project(values):
        half = n_head // 2 * (rows // per)
        return pl.pallas_call(
            functools.partial(project_kernel, n_tok, per, groups),
            in_specs=[vmem] * (n_tok + 1),
            out_specs=[vmem] * (2 * len(groups)),
            out_shape=[
                pltpu.VMEM((half, tile * count), bf16) for _, _, count, _ in groups for _ in "sk"
            ],
            scratch_shapes=[pltpu.VMEM((2 * half, depth), bf16)],
            compiler_params=params,
            name="project",
            cost_estimate=cost(4 * half * depth * columns),
        )(*values, in_vmem(w_o))

    def scatter(send, keep, bits):
        for at, bit in enumerate(bits):
            got = xor_permute(send, "head", bit)
            if at == len(bits) - 1:
                return keep.astype(f32) + got.astype(f32)
            half = keep.shape[0] // 2
            send = (keep[:half].astype(f32) + got[:half].astype(f32)).astype(bf16)
            keep = (keep[half:].astype(f32) + got[half:].astype(f32)).astype(bf16)

    out = []
    for which in range(CHUNKS):
        parts = project(gather(rest(which)))
        out.append(
            jnp.concatenate(
                [
                    scatter(parts[2 * j], parts[2 * j + 1], bits).astype(bf16)
                    for j, (bits, _, _, _) in enumerate(groups)
                ],
                1,
            )
        )
    return jnp.concatenate(out, 0)


def solution(mesh):
    return jax.shard_map(
        shards,
        mesh=mesh,
        in_specs=(
            P("tok", "head"),
            P("tok", "head"),
            P("tok", None),
            P("tok", None),
            P(None, "head"),
            P(None, "head"),
            P("head", "tok"),
            P(),
        ),
        out_specs=P("head", "tok"),
        check_vma=False,
    )
```

time: 152 us -> 73 us (0.48)
  waiting for transfers between devices: 101 us -> 24.6 us
  starting transfers between devices: 0.09 us -> 26.1 us
  matrix products: 24.6 us -> 0 us
  Pallas kernels: 0 us -> 20.2 us
  between operations: 13.9 us -> 0.89 us
  local copies, waits for them, and re-layouts: 6.77 us -> 0.03 us
  other arithmetic: 5.22 us -> 1.11 us
    reduce_scatter x1 -> x0, waiting for transfers between devices: 66.5 us -> none  [shards(): lax.psum_scatter(partial_rows.astype(jnp.bfloat16), 'head', scatter_dimen...]
    all_gather x2 -> x0, waiting for transfers between devices: 34.4 us -> none  [the longest x1 22.9 us: shards(): lax.all_gather(value_out, 'tok', axis=0, tiled=True)]
    ppermute x0 -> x24, starting transfers between devices: none -> 26.1 us  [xor_permute(): return lax.ppermute(x, axis, [(i, i ^ bit) for i in range(n)])]
    ppermute x0 -> x24, waiting for transfers between devices: none -> 24.6 us  [xor_permute(): return lax.ppermute(x, axis, [(i, i ^ bit) for i in range(n)])]
    dot_general x6 -> x0, matrix products: 24.6 us -> none  [the longest x1 8.98 us: shards(): jnp.dot(lax.all_gather(value_out, 'tok', axis=0, tiled=True), w_o, prefer...]
    pallas_call x0 -> x6, Pallas kernels: none -> 20.2 us  [the longest x2 9.05 us: rest(): pl.pallas_call(functools.partial(rest_kernel, far, tokens, group, which),...]
    reshape x2 -> x0, local copies, waits for them, and re-layouts: 4.27 us -> none  [the longest x1 3.93 us: shards(): w_uv.reshape(KVL, head_count, DV)]
    reduce_sum x1 -> x0, other arithmetic: 3.3 us -> none  [shards(): weight_sum = jnp.sum(weights, axis=1)]
  transfers between devices with their start and end apart: 3 -> 24, of which waited for: 3 -> 11; matrix products, arithmetic and copies ran while one was open for 6% -> 1% of each run, Pallas kernels for 0% -> 21%
where the time goes in v1:
time: 73 us; the launch traced here: 72.8 us
  starting transfers between devices  26.1 us (36%)
  waiting for transfers between devices  24.6 us (34%)
  Pallas kernels  20.2 us (28%)
  other arithmetic  1.11 us (2%)
  between operations  0.89 us (1%)
    ppermute x24, starting transfers between devices, xor_permute(): return lax.ppermute(x, axis, [(i, i ^ bit) for i in range(n)])  26.1 us
    ppermute x24, waiting for transfers between devices, xor_permute(): return lax.ppermute(x, axis, [(i, i ^ bit) for i in range(n)])  24.6 us
    pallas_call x2, Pallas kernels, rest(): pl.pallas_call(functools.partial(rest_kernel, far, tokens, group, which),...  9.05 us
    pallas_call x2, Pallas kernels, project(): pl.pallas_call(functools.partial(project_kernel, n_tok, per, groups), in_...  4.41 us
    pallas_call x1, Pallas kernels, shards(): pl.pallas_call(functools.partial(local_kernel, near, tokens, group), in_s...  4.12 us
    pallas_call x1, Pallas kernels, shards(): pl.pallas_call(functools.partial(query_kernel, tokens, group), in_specs=[...  2.59 us
  transfers between devices with their start and end apart: 24, of which 11 were waited for; matrix products, arithmetic and copies ran while one was open for 1% of the time, Pallas kernels for 21%

profile of v1, /device:TPU:0, one launch (start us, length us, event | category | flops | bytes accessed | tf_op | source)
XLA Modules:
  0.0 72.8 jit_solution(16636532614221774199)
XLA Ops:
  0.5 2.9 %collective-permute-start = (bf16[576,128]{1,0:T(8,128)(2,1)}, bf16[576,128]{1,0:T(8,128)(2,1)S(1)}, u32[]{:S(2)}, u32[]{:S(2)}) collective-permute-start(bf16[576,128]{1,0:T(8,128)(2,1)} %bitcast.5), channel_id=1, source_target_pairs={{0,16},{8,24},{16,0},{24,8},{1,17},{9,25},{17,1},{25,9},{2,18},{10... | collective-permute-start | bytes 442376 | tf_op jit(solution)/shard_map/ppermute | solution.py:38
  4.2 2.6 %query_latent.1.refs_1_ = bf16[2,16,64,576]{3,2,1,0:T(8,128)(2,1)S(1)} custom-call(bf16[128,2048]{1,0:T(8,128)(2,1)} %qn.1, bf16[128,1024]{1,0:T(8,128)(2,1)} %qr.1, bf16[512,2048]{1,0:T(8,128)(2,1)} %wuk.1), custom_call_target="tpu_custom_call" | custom-call | flops 268435456 | tf_op jit(solution)/shard_map/query_latent/pallas_call | solution.py:271
  6.8 4.1 %local_keys.1 = (f32[2,16,64,512]{3,2,1,0:T(8,128)S(1)}, f32[2,16,64,128]{3,2,1,0:T(8,128)S(1)}) custom-call(s32[1]{0:T(128)S(6)} %copy.9.refs_0_, bf16[2,16,64,576]{3,2,1,0:T(8,128)(2,1)S(1)} %query_latent.1.refs_1_, bf16[576,128]{1,0:T(8,128)(2,1)S(1)} %bitcast.6, bf16[576,128]{1,0:T(8,128)(2,1)S(1)} %collective-permute-done.2.refs_3_, ...), custom_call_target="tpu_custom_call" | custom-call | flops 2415919104 | tf_op jit(solution)/shard_map/local_keys/pallas_call | solution.py:288
  12.6 4.5 %far_keys.2.refs_0_ = bf16[64,2048]{1,0:T(8,128)(2,1)S(1)} custom-call(s32[1]{0:T(128)S(6)} %copy.9.refs_0_, bf16[2,16,64,576]{3,2,1,0:T(8,128)(2,1)S(1)} %query_latent.1.refs_1_, f32[2,16,64,512]{3,2,1,0:T(8,128)S(1)} %get-tuple-element.21.refs_2_, f32[2,16,64,128]{3,2,1,0:T(8,128)S(1)} %get-tuple-element.22.refs_3_, bf16[512,2048]{1,0:T(8,128)(2,1)S(1)} %copy-done, ...), custom_call_target="tpu_custom_call" | custom-call | flops 1207959552 | tf_op jit(solution)/shard_map/far_keys/pallas_call | solution.py:310
  17.2 2.1 %collective-permute-start.7 = (bf16[64,2048]{1,0:T(8,128)(2,1)S(1)}, bf16[64,2048]{1,0:T(8,128)(2,1)S(1)}, u32[]{:S(2)}, u32[]{:S(2)}) collective-permute-start(bf16[64,2048]{1,0:T(8,128)(2,1)S(1)} %far_keys.2.refs_0_), channel_id=1, source_target_pairs={{0,16},{8,24},{16,0},{24,8},{1,17},{9,25},{17,1},{25,9},{2,18},{10... | collective-permute-start | bytes 786440 | tf_op jit(solution)/shard_map/ppermute | solution.py:38
  19.2 4.5 %far_keys.3.refs_0_ = bf16[64,2048]{1,0:T(8,128)(2,1)S(1)} custom-call(s32[1]{0:T(128)S(6)} %copy.9.refs_0_, bf16[2,16,64,576]{3,2,1,0:T(8,128)(2,1)S(1)} %query_latent.1.refs_1_, f32[2,16,64,512]{3,2,1,0:T(8,128)S(1)} %get-tuple-element.21.refs_2_, f32[2,16,64,128]{3,2,1,0:T(8,128)S(1)} %get-tuple-element.22.refs_3_, bf16[512,2048]{1,0:T(8,128)(2,1)S(1)} %copy-done, ...), custom_call_target="tpu_custom_call" | custom-call | flops 1207959552 | tf_op jit(solution)/shard_map/far_keys/pallas_call | solution.py:310
  23.9 2.1 %collective-permute-done.7.refs_2_ = bf16[64,2048]{1,0:T(8,128)(2,1)S(1)} collective-permute-done((bf16[64,2048]{1,0:T(8,128)(2,1)S(1)}, bf16[64,2048]{1,0:T(8,128)(2,1)S(1)}, u32[]{:S(2)}, u32[]{:S(2)}) %collective-permute-start.7) | collective-permute-done | bytes 262176 | tf_op jit(solution)/shard_map/ppermute | solution.py:38
  26.5 5.5 %collective-permute-done.16.refs_2_ = bf16[64,2048]{1,0:T(8,128)(2,1)S(1)} collective-permute-done((bf16[64,2048]{1,0:T(8,128)(2,1)S(1)}, bf16[64,2048]{1,0:T(8,128)(2,1)S(1)}, u32[]{:S(2)}, u32[]{:S(2)}) %collective-permute-start.16) | collective-permute-done | bytes 262176 | tf_op jit(solution)/shard_map/ppermute | solution.py:38
  32.1 2.2 %project.2 = (bf16[128,1280]{1,0:T(8,128)(2,1)S(1)}, bf16[128,1280]{1,0:T(8,128)(2,1)S(1)}, bf16[128,512]{1,0:T(8,128)(2,1)S(1)}, bf16[128,512]{1,0:T(8,128)(2,1)S(1)}) custom-call(bf16[64,2048]{1,0:T(8,128)(2,1)S(1)} %far_keys.2.refs_0_, bf16[64,2048]{1,0:T(8,128)(2,1)S(1)} %collective-permute-done.6.refs_1_, ...), custom_call_target="tpu_custom_call" | custom-call | flops 1879048192 | tf_op jit(solution)/shard_map/project/pallas_call | solution.py:333
  34.3 1.6 %collective-permute-start.12 = (bf16[128,512]{1,0:T(8,128)(2,1)S(1)}, bf16[128,512]{1,0:T(8,128)(2,1)S(1)}, u32[]{:S(2)}, u32[]{:S(2)}) collective-permute-start(bf16[128,512]{1,0:T(8,128)(2,1)S(1)} %get-tuple-element.28), channel_id=1, source_target_pairs={{0,2},{1,3},{2,0},{3,1},{4,6},{5,7},{6,4},{7,5},{8,10},{9,11},{10,... | collective-permute-start | bytes 393224 | tf_op jit(solution)/shard_map/ppermute | solution.py:38
  36.0 2.2 %project.3 = (bf16[128,1280]{1,0:T(8,128)(2,1)S(1)}, bf16[128,1280]{1,0:T(8,128)(2,1)S(1)}, bf16[128,512]{1,0:T(8,128)(2,1)S(1)}, bf16[128,512]{1,0:T(8,128)(2,1)S(1)}) custom-call(bf16[64,2048]{1,0:T(8,128)(2,1)S(1)} %far_keys.3.refs_0_, bf16[64,2048]{1,0:T(8,128)(2,1)S(1)} %collective-permute-done.15.refs_1_, ...), custom_call_target="tpu_custom_call" | custom-call | flops 1879048192 | tf_op jit(solution)/shard_map/project/pallas_call | solution.py:333
  38.7 1.5 %collective-permute-start.18 = (bf16[128,1280]{1,0:T(8,128)(2,1)S(1)}, bf16[128,1280]{1,0:T(8,128)(2,1)S(1)}, u32[]{:S(2)}, u32[]{:S(2)}) collective-permute-start(bf16[128,1280]{1,0:T(8,128)(2,1)S(1)} %get-tuple-element.30), channel_id=1, source_target_pairs={{0,1},{1,0},{2,3},{3,2},{4,5},{5,4},{6,7},{7,6},{8,9},{9,8},{10,11... | collective-permute-start | bytes 983048 | tf_op jit(solution)/shard_map/ppermute | solution.py:38
  40.7 2.7 %collective-permute-start.13 = (bf16[64,512]{1,0:T(8,128)(2,1)S(1)}, bf16[64,512]{1,0:T(8,128)(2,1)S(1)}, u32[]{:S(2)}, u32[]{:S(2)}) collective-permute-start(bf16[64,512]{1,0:T(8,128)(2,1)S(1)} %get-tuple-element.38), channel_id=1, source_target_pairs={{0,4},{1,5},{2,6},{3,7},{4,0},{5,1},{6,2},{7,3},{8,12},{9,13},{10,... | collective-permute-start | bytes 196616 | tf_op jit(solution)/shard_map/ppermute | solution.py:38
  43.4 1.1 %collective-permute-done.21 = bf16[128,512]{1,0:T(8,128)(2,1)S(1)} collective-permute-done((bf16[128,512]{1,0:T(8,128)(2,1)S(1)}, bf16[128,512]{1,0:T(8,128)(2,1)S(1)}, u32[]{:S(2)}, u32[]{:S(2)}) %collective-permute-start.21) | collective-permute-done | bytes 131104 | tf_op jit(solution)/shard_map/ppermute | solution.py:38
  44.6 2.7 %collective-permute-start.22 = (bf16[64,512]{1,0:T(8,128)(2,1)S(1)}, bf16[64,512]{1,0:T(8,128)(2,1)S(1)}, u32[]{:S(2)}, u32[]{:S(2)}) collective-permute-start(bf16[64,512]{1,0:T(8,128)(2,1)S(1)} %get-tuple-element.40), channel_id=1, source_target_pairs={{0,4},{1,5},{2,6},{3,7},{4,0},{5,1},{6,2},{7,3},{8,12},{9,13},{10,... | collective-permute-start | bytes 196616 | tf_op jit(solution)/shard_map/ppermute | solution.py:38
  47.3 1.6 %collective-permute-start.14 = (bf16[32,512]{1,0:T(8,128)(2,1)S(1)}, bf16[32,512]{1,0:T(8,128)(2,1)S(1)}, u32[]{:S(2)}, u32[]{:S(2)}) collective-permute-start(bf16[32,512]{1,0:T(8,128)(2,1)S(1)} %add_convert_fusion.18), channel_id=1, source_target_pairs={{0,1},{1,0},{2,3},{3,2},{4,5},{5,4},{6,7},{7,6},{8,9},{9,8},{10,11... | collective-permute-start | bytes 98312 | tf_op jit(solution)/shard_map/ppermute | solution.py:38
  48.8 1.6 %collective-permute-done.22 = bf16[64,512]{1,0:T(8,128)(2,1)S(1)} collective-permute-done((bf16[64,512]{1,0:T(8,128)(2,1)S(1)}, bf16[64,512]{1,0:T(8,128)(2,1)S(1)}, u32[]{:S(2)}, u32[]{:S(2)}) %collective-permute-start.22) | collective-permute-done | bytes 65568 | tf_op jit(solution)/shard_map/ppermute | solution.py:38
  50.4 1.6 %collective-permute-start.23 = (bf16[32,512]{1,0:T(8,128)(2,1)S(1)}, bf16[32,512]{1,0:T(8,128)(2,1)S(1)}, u32[]{:S(2)}, u32[]{:S(2)}) collective-permute-start(bf16[32,512]{1,0:T(8,128)(2,1)S(1)} %add_convert_fusion.15), channel_id=1, source_target_pairs={{0,1},{1,0},{2,3},{3,2},{4,5},{5,4},{6,7},{7,6},{8,9},{9,8},{10,11... | collective-permute-start | bytes 98312 | tf_op jit(solution)/shard_map/ppermute | solution.py:38
  52.0 4.3 %collective-permute-done.14 = bf16[32,512]{1,0:T(8,128)(2,1)S(1)} collective-permute-done((bf16[32,512]{1,0:T(8,128)(2,1)S(1)}, bf16[32,512]{1,0:T(8,128)(2,1)S(1)}, u32[]{:S(2)}, u32[]{:S(2)}) %collective-permute-start.14) | collective-permute-done | bytes 32800 | tf_op jit(solution)/shard_map/ppermute | solution.py:38
  56.8 1.6 %collective-permute-start.19 = (bf16[64,1280]{1,0:T(8,128)(2,1)S(1)}, bf16[64,1280]{1,0:T(8,128)(2,1)S(1)}, u32[]{:S(2)}, u32[]{:S(2)}) collective-permute-start(bf16[64,1280]{1,0:T(8,128)(2,1)S(1)} %get-tuple-element.36), channel_id=1, source_target_pairs={{0,2},{1,3},{2,0},{3,1},{4,6},{5,7},{6,4},{7,5},{8,10},{9,11},{10,... | collective-permute-start | bytes 491528 | tf_op jit(solution)/shard_map/ppermute | solution.py:38
  59.0 5.6 %collective-permute-done.19 = bf16[64,1280]{1,0:T(8,128)(2,1)S(1)} collective-permute-done((bf16[64,1280]{1,0:T(8,128)(2,1)S(1)}, bf16[64,1280]{1,0:T(8,128)(2,1)S(1)}, u32[]{:S(2)}, u32[]{:S(2)}) %collective-permute-start.19) | collective-permute-done | bytes 163872 | tf_op jit(solution)/shard_map/ppermute | solution.py:38
  64.7 2.0 %collective-permute-start.20 = (bf16[32,1280]{1,0:T(8,128)(2,1)S(1)}, bf16[32,1280]{1,0:T(8,128)(2,1)S(1)}, u32[]{:S(2)}, u32[]{:S(2)}) collective-permute-start(bf16[32,1280]{1,0:T(8,128)(2,1)S(1)} %add_convert_fusion.5), channel_id=1, source_target_pairs={{0,4},{1,5},{2,6},{3,7},{4,0},{5,1},{6,2},{7,3},{8,12},{9,13},{10,... | collective-permute-start | bytes 245768 | tf_op jit(solution)/shard_map/ppermute | solution.py:38
  66.7 2.5 %collective-permute-start.11 = (bf16[32,1280]{1,0:T(8,128)(2,1)S(1)}, bf16[32,1280]{1,0:T(8,128)(2,1)S(1)}, u32[]{:S(2)}, u32[]{:S(2)}) collective-permute-start(bf16[32,1280]{1,0:T(8,128)(2,1)S(1)} %add_convert_fusion.8), channel_id=1, source_target_pairs={{0,4},{1,5},{2,6},{3,7},{4,0},{5,1},{6,2},{7,3},{8,12},{9,13},{10,... | collective-permute-start | bytes 245768 | tf_op jit(solution)/shard_map/ppermute | solution.py:38
  69.2 1.9 %collective-permute-done.20 = bf16[32,1280]{1,0:T(8,128)(2,1)S(1)} collective-permute-done((bf16[32,1280]{1,0:T(8,128)(2,1)S(1)}, bf16[32,1280]{1,0:T(8,128)(2,1)S(1)}, u32[]{:S(2)}, u32[]{:S(2)}) %collective-permute-start.20) | collective-permute-done | bytes 81952 | tf_op jit(solution)/shard_map/ppermute | solution.py:38
  (54 shorter events, 6.9 us)
Async XLA Ops:
  0.0 6.8 %collective-permute-start.2 = (bf16[576,128]{1,0:T(8,128)(2,1)}, bf16[576,128]{1,0:T(8,128)(2,1)S(1)}, u32[]{:S(2)}, u32[]{:S(2)}) collective-permute-start(bf16[576,128]{1,0:T(8,128)(2,1)} %bitcast.4), channel_id=1, source_target_pairs={{0,8},{8,0},{16,24},{24,16},{1,9},{9,1},{17,25},{25,17},{2,10},{10... | collective-permute-start | bytes 442376 | tf_op jit(solution)/shard_map/ppermute | solution.py:38
  0.5 6.3 %collective-permute-start.3 = (bf16[576,128]{1,0:T(8,128)(2,1)}, bf16[576,128]{1,0:T(8,128)(2,1)S(1)}, u32[]{:S(2)}, u32[]{:S(2)}) collective-permute-start(bf16[576,128]{1,0:T(8,128)(2,1)} %bitcast.7), channel_id=1, source_target_pairs={{0,8},{8,0},{16,24},{24,16},{1,9},{9,1},{17,25},{25,17},{2,10},{10... | collective-permute-start | bytes 442376 | tf_op jit(solution)/shard_map/ppermute | solution.py:38
  0.5 10.4 %collective-permute-start = (bf16[576,128]{1,0:T(8,128)(2,1)}, bf16[576,128]{1,0:T(8,128)(2,1)S(1)}, u32[]{:S(2)}, u32[]{:S(2)}) collective-permute-start(bf16[576,128]{1,0:T(8,128)(2,1)} %bitcast.5), channel_id=1, source_target_pairs={{0,16},{8,24},{16,0},{24,8},{1,17},{9,25},{17,1},{25,9},{2,18},{10... | collective-permute-start | bytes 442376 | tf_op jit(solution)/shard_map/ppermute | solution.py:38
  3.5 7.5 %collective-permute-start.1 = (bf16[576,128]{1,0:T(8,128)(2,1)}, bf16[576,128]{1,0:T(8,128)(2,1)S(1)}, u32[]{:S(2)}, u32[]{:S(2)}) collective-permute-start(bf16[576,128]{1,0:T(8,128)(2,1)} %bitcast.8), channel_id=1, source_target_pairs={{0,16},{8,24},{16,0},{24,8},{1,17},{9,25},{17,1},{25,9},{2,18},{10... | collective-permute-start | bytes 442376 | tf_op jit(solution)/shard_map/ppermute | solution.py:38
  11.0 1.4 %collective-permute-start.4 = (bf16[576,128]{1,0:T(8,128)(2,1)S(1)}, bf16[576,128]{1,0:T(8,128)(2,1)S(1)}, u32[]{:S(2)}, u32[]{:S(2)}) collective-permute-start(bf16[576,128]{1,0:T(8,128)(2,1)S(1)} %collective-permute-done.refs_5_), channel_id=1, source_target_pairs={{0,8},{8,0},{16,24},{24,16},{1,9},{9,1},{17,25},{25,17},{2,10},{10... | collective-permute-start | bytes 442376 | tf_op jit(solution)/shard_map/ppermute | solution.py:38
  11.0 1.6 %collective-permute-start.5 = (bf16[576,128]{1,0:T(8,128)(2,1)S(1)}, bf16[576,128]{1,0:T(8,128)(2,1)S(1)}, u32[]{:S(2)}, u32[]{:S(2)}) collective-permute-start(bf16[576,128]{1,0:T(8,128)(2,1)S(1)} %collective-permute-done.1.refs_7_), channel_id=1, source_target_pairs={{0,8},{8,0},{16,24},{24,16},{1,9},{9,1},{17,25},{25,17},{2,10},{10... | collective-permute-start | bytes 442376 | tf_op jit(solution)/shard_map/ppermute | solution.py:38
  17.2 8.8 %collective-permute-start.7 = (bf16[64,2048]{1,0:T(8,128)(2,1)S(1)}, bf16[64,2048]{1,0:T(8,128)(2,1)S(1)}, u32[]{:S(2)}, u32[]{:S(2)}) collective-permute-start(bf16[64,2048]{1,0:T(8,128)(2,1)S(1)} %far_keys.2.refs_0_), channel_id=1, source_target_pairs={{0,16},{8,24},{16,0},{24,8},{1,17},{9,25},{17,1},{25,9},{2,18},{10... | collective-permute-start | bytes 786440 | tf_op jit(solution)/shard_map/ppermute | solution.py:38
  23.8 8.3 %collective-permute-start.16 = (bf16[64,2048]{1,0:T(8,128)(2,1)S(1)}, bf16[64,2048]{1,0:T(8,128)(2,1)S(1)}, u32[]{:S(2)}, u32[]{:S(2)}) collective-permute-start(bf16[64,2048]{1,0:T(8,128)(2,1)S(1)} %far_keys.3.refs_0_), channel_id=1, source_target_pairs={{0,16},{8,24},{16,0},{24,8},{1,17},{9,25},{17,1},{25,9},{2,18},{10... | collective-permute-start | bytes 786440 | tf_op jit(solution)/shard_map/ppermute | solution.py:38
  23.9 8.2 %collective-permute-start.6 = (bf16[64,2048]{1,0:T(8,128)(2,1)S(1)}, bf16[64,2048]{1,0:T(8,128)(2,1)S(1)}, u32[]{:S(2)}, u32[]{:S(2)}) collective-permute-start(bf16[64,2048]{1,0:T(8,128)(2,1)S(1)} %far_keys.2.refs_0_), channel_id=1, source_target_pairs={{0,8},{8,0},{16,24},{24,16},{1,9},{9,1},{17,25},{25,17},{2,10},{10... | collective-permute-start | bytes 786440 | tf_op jit(solution)/shard_map/ppermute | solution.py:38
  26.0 6.1 %collective-permute-start.8 = (bf16[64,2048]{1,0:T(8,128)(2,1)S(1)}, bf16[64,2048]{1,0:T(8,128)(2,1)S(1)}, u32[]{:S(2)}, u32[]{:S(2)}) collective-permute-start(bf16[64,2048]{1,0:T(8,128)(2,1)S(1)} %collective-permute-done.7.refs_2_), channel_id=1, source_target_pairs={{0,8},{8,0},{16,24},{24,16},{1,9},{9,1},{17,25},{25,17},{2,10},{10... | collective-permute-start | bytes 786440 | tf_op jit(solution)/shard_map/ppermute | solution.py:38
  26.0 10.0 %collective-permute-start.15 = (bf16[64,2048]{1,0:T(8,128)(2,1)S(1)}, bf16[64,2048]{1,0:T(8,128)(2,1)S(1)}, u32[]{:S(2)}, u32[]{:S(2)}) collective-permute-start(bf16[64,2048]{1,0:T(8,128)(2,1)S(1)} %far_keys.3.refs_0_), channel_id=1, source_target_pairs={{0,8},{8,0},{16,24},{24,16},{1,9},{9,1},{17,25},{25,17},{2,10},{10... | collective-permute-start | bytes 786440 | tf_op jit(solution)/shard_map/ppermute | solution.py:38
  32.0 3.9 %collective-permute-start.17 = (bf16[64,2048]{1,0:T(8,128)(2,1)S(1)}, bf16[64,2048]{1,0:T(8,128)(2,1)S(1)}, u32[]{:S(2)}, u32[]{:S(2)}) collective-permute-start(bf16[64,2048]{1,0:T(8,128)(2,1)S(1)} %collective-permute-done.16.refs_2_), channel_id=1, source_target_pairs={{0,8},{8,0},{16,24},{24,16},{1,9},{9,1},{17,25},{25,17},{2,10},{10... | collective-permute-start | bytes 786440 | tf_op jit(solution)/shard_map/ppermute | solution.py:38
  34.3 6.4 %collective-permute-start.12 = (bf16[128,512]{1,0:T(8,128)(2,1)S(1)}, bf16[128,512]{1,0:T(8,128)(2,1)S(1)}, u32[]{:S(2)}, u32[]{:S(2)}) collective-permute-start(bf16[128,512]{1,0:T(8,128)(2,1)S(1)} %get-tuple-element.28), channel_id=1, source_target_pairs={{0,2},{1,3},{2,0},{3,1},{4,6},{5,7},{6,4},{7,5},{8,10},{9,11},{10,... | collective-permute-start | bytes 393224 | tf_op jit(solution)/shard_map/ppermute | solution.py:38
  38.2 6.4 %collective-permute-start.21 = (bf16[128,512]{1,0:T(8,128)(2,1)S(1)}, bf16[128,512]{1,0:T(8,128)(2,1)S(1)}, u32[]{:S(2)}, u32[]{:S(2)}) collective-permute-start(bf16[128,512]{1,0:T(8,128)(2,1)S(1)} %get-tuple-element.32), channel_id=1, source_target_pairs={{0,2},{1,3},{2,0},{3,1},{4,6},{5,7},{6,4},{7,5},{8,10},{9,11},{10,... | collective-permute-start | bytes 393224 | tf_op jit(solution)/shard_map/ppermute | solution.py:38
  38.7 18.0 %collective-permute-start.18 = (bf16[128,1280]{1,0:T(8,128)(2,1)S(1)}, bf16[128,1280]{1,0:T(8,128)(2,1)S(1)}, u32[]{:S(2)}, u32[]{:S(2)}) collective-permute-start(bf16[128,1280]{1,0:T(8,128)(2,1)S(1)} %get-tuple-element.30), channel_id=1, source_target_pairs={{0,1},{1,0},{2,3},{3,2},{4,5},{5,4},{6,7},{7,6},{8,9},{9,8},{10,11... | collective-permute-start | bytes 983048 | tf_op jit(solution)/shard_map/ppermute | solution.py:38
  40.2 18.2 %collective-permute-start.9 = (bf16[128,1280]{1,0:T(8,128)(2,1)S(1)}, bf16[128,1280]{1,0:T(8,128)(2,1)S(1)}, u32[]{:S(2)}, u32[]{:S(2)}) collective-permute-start(bf16[128,1280]{1,0:T(8,128)(2,1)S(1)} %get-tuple-element.26), channel_id=1, source_target_pairs={{0,1},{1,0},{2,3},{3,2},{4,5},{5,4},{6,7},{7,6},{8,9},{9,8},{10,11... | collective-permute-start | bytes 983048 | tf_op jit(solution)/shard_map/ppermute | solution.py:38
  40.7 6.5 %collective-permute-start.13 = (bf16[64,512]{1,0:T(8,128)(2,1)S(1)}, bf16[64,512]{1,0:T(8,128)(2,1)S(1)}, u32[]{:S(2)}, u32[]{:S(2)}) collective-permute-start(bf16[64,512]{1,0:T(8,128)(2,1)S(1)} %get-tuple-element.38), channel_id=1, source_target_pairs={{0,4},{1,5},{2,6},{3,7},{4,0},{5,1},{6,2},{7,3},{8,12},{9,13},{10,... | collective-permute-start | bytes 196616 | tf_op jit(solution)/shard_map/ppermute | solution.py:38
  44.6 5.8 %collective-permute-start.22 = (bf16[64,512]{1,0:T(8,128)(2,1)S(1)}, bf16[64,512]{1,0:T(8,128)(2,1)S(1)}, u32[]{:S(2)}, u32[]{:S(2)}) collective-permute-start(bf16[64,512]{1,0:T(8,128)(2,1)S(1)} %get-tuple-element.40), channel_id=1, source_target_pairs={{0,4},{1,5},{2,6},{3,7},{4,0},{5,1},{6,2},{7,3},{8,12},{9,13},{10,... | collective-permute-start | bytes 196616 | tf_op jit(solution)/shard_map/ppermute | solution.py:38
  47.3 9.0 %collective-permute-start.14 = (bf16[32,512]{1,0:T(8,128)(2,1)S(1)}, bf16[32,512]{1,0:T(8,128)(2,1)S(1)}, u32[]{:S(2)}, u32[]{:S(2)}) collective-permute-start(bf16[32,512]{1,0:T(8,128)(2,1)S(1)} %add_convert_fusion.18), channel_id=1, source_target_pairs={{0,1},{1,0},{2,3},{3,2},{4,5},{5,4},{6,7},{7,6},{8,9},{9,8},{10,11... | collective-permute-start | bytes 98312 | tf_op jit(solution)/shard_map/ppermute | solution.py:38
  50.4 6.2 %collective-permute-start.23 = (bf16[32,512]{1,0:T(8,128)(2,1)S(1)}, bf16[32,512]{1,0:T(8,128)(2,1)S(1)}, u32[]{:S(2)}, u32[]{:S(2)}) collective-permute-start(bf16[32,512]{1,0:T(8,128)(2,1)S(1)} %add_convert_fusion.15), channel_id=1, source_target_pairs={{0,1},{1,0},{2,3},{3,2},{4,5},{5,4},{6,7},{7,6},{8,9},{9,8},{10,11... | collective-permute-start | bytes 98312 | tf_op jit(solution)/shard_map/ppermute | solution.py:38
  56.8 7.9 %collective-permute-start.19 = (bf16[64,1280]{1,0:T(8,128)(2,1)S(1)}, bf16[64,1280]{1,0:T(8,128)(2,1)S(1)}, u32[]{:S(2)}, u32[]{:S(2)}) collective-permute-start(bf16[64,1280]{1,0:T(8,128)(2,1)S(1)} %get-tuple-element.36), channel_id=1, source_target_pairs={{0,2},{1,3},{2,0},{3,1},{4,6},{5,7},{6,4},{7,5},{8,10},{9,11},{10,... | collective-permute-start | bytes 491528 | tf_op jit(solution)/shard_map/ppermute | solution.py:38
  58.5 8.2 %collective-permute-start.10 = (bf16[64,1280]{1,0:T(8,128)(2,1)S(1)}, bf16[64,1280]{1,0:T(8,128)(2,1)S(1)}, u32[]{:S(2)}, u32[]{:S(2)}) collective-permute-start(bf16[64,1280]{1,0:T(8,128)(2,1)S(1)} %get-tuple-element.34), channel_id=1, source_target_pairs={{0,2},{1,3},{2,0},{3,1},{4,6},{5,7},{6,4},{7,5},{8,10},{9,11},{10,... | collective-permute-start | bytes 491528 | tf_op jit(solution)/shard_map/ppermute | solution.py:38
  64.7 6.4 %collective-permute-start.20 = (bf16[32,1280]{1,0:T(8,128)(2,1)S(1)}, bf16[32,1280]{1,0:T(8,128)(2,1)S(1)}, u32[]{:S(2)}, u32[]{:S(2)}) collective-permute-start(bf16[32,1280]{1,0:T(8,128)(2,1)S(1)} %add_convert_fusion.5), channel_id=1, source_target_pairs={{0,4},{1,5},{2,6},{3,7},{4,0},{5,1},{6,2},{7,3},{8,12},{9,13},{10,... | collective-permute-start | bytes 245768 | tf_op jit(solution)/shard_map/ppermute | solution.py:38
  66.7 5.4 %collective-permute-start.11 = (bf16[32,1280]{1,0:T(8,128)(2,1)S(1)}, bf16[32,1280]{1,0:T(8,128)(2,1)S(1)}, u32[]{:S(2)}, u32[]{:S(2)}) collective-permute-start(bf16[32,1280]{1,0:T(8,128)(2,1)S(1)} %add_convert_fusion.8), channel_id=1, source_target_pairs={{0,4},{1,5},{2,6},{3,7},{4,0},{5,1},{6,2},{7,3},{8,12},{9,13},{10,... | collective-permute-start | bytes 245768 | tf_op jit(solution)/shard_map/ppermute | solution.py:38
  (5 other events, 45.5 us)

commit v2 on v1

v2 whole, which is shorter than its diff:
```python
import functools
import math

import jax
import jax.numpy as jnp
from jax import lax
from jax.experimental import pallas as pl
from jax.experimental.pallas import tpu as pltpu
from jax.sharding import PartitionSpec as P

DN = 128
DR = 64
DV = 128
KVL = 512
KD = KVL + DR
LANES = 128
KQ = KD + LANES - KD % LANES

MASKED = -1e30
CHUNKS = 2
PLAN = (
    (0.57, lambda bits: [(b,) for b in bits]),
    (0.43, lambda bits: [(b,) for b in bits[1:] + bits[:1]]),
)
COST_SHARE = 1
VMEM_LIMIT = 24 * 1024 * 1024
EXP_SCALE = math.log2(math.e) / math.sqrt(DN + DR)

f32 = jnp.float32
bf16 = jnp.bfloat16


def dot(a, b):
    return jnp.dot(a, b, preferred_element_type=f32)


def dot_t(a, b):
    return lax.dot_general(a, b, (((1,), (1,)), ((), ())), preferred_element_type=f32)


def xor_permute(x, axis, bit):
    n = lax.axis_size(axis)
    return lax.ppermute(x, axis, [(i, i ^ bit) for i in range(n)])


def bits_of(n):
    return [1 << i for i in range(n.bit_length() - 1)]


def in_vmem(x):
    return pltpu.with_memory_space_constraint(x, pltpu.VMEM)


def load_keys(caches, spans, rels, limit, tokens, kt, k):
    me = lax.axis_index("tok")
    cached = caches[0].shape[1]
    size = cached + tokens
    tail = KQ - KD
    first = lax.broadcasted_iota(jnp.int32, (tail, 1), 0) == 0

    def mask(dead):
        return jnp.where(first & dead, MASKED, 0.0).astype(bf16)

    for at, (cache, span, rel) in enumerate(zip(caches, spans, rels)):
        owner = me ^ rel
        start, middle, end = at * size, at * size + cached, (at + 1) * size
        kt[:KD, start:middle] = cache[...]
        kt[:KD, middle:end] = span[...]
        column = lax.broadcasted_iota(jnp.int32, (tail, cached), 1)
        kt[KD:, start:middle] = mask(owner * cached + column >= limit)
        column = lax.broadcasted_iota(jnp.int32, (tail, tokens), 1)
        kt[KD:, middle:end] = mask(owner * tokens + 0 * column > me * tokens)
    k[...] = kt[:KVL, :].T


def lanes(x):
    return [x[:, j : j + LANES] for j in range(0, x.shape[1], LANES)]


def pipelined(count, scores, finish):
    ahead = scores(0)
    for i in range(count):
        now, ahead = ahead, scores(i + 1) if i + 1 < count else None
        finish(i, now)


def softmax(s, top):
    tiles = lanes(s)
    most = functools.reduce(jnp.maximum, tiles)
    new = jnp.broadcast_to(jnp.max(most, axis=1, keepdims=True), most.shape)
    if top is not None:
        new = jnp.maximum(top, new)
    p = [jnp.exp2((x - new) * EXP_SCALE) for x in tiles]
    total = jnp.sum(functools.reduce(jnp.add, p), axis=1, keepdims=True)
    return jnp.concatenate([x.astype(bf16) for x in p], 1), total, new


def split_refs(refs, *counts):
    out, at = [], 0
    for count in counts:
        out.append(refs[at : at + count])
        at += count
    return out + [refs[at:]]


def query_kernel(tokens, group, qn, qr, wuk, q_out, nope, rotary, up, sems):
    half = tokens // 2
    part = half // CHUNKS
    rows = tokens // CHUNKS
    steps = q_out.shape[1] // group

    def copies(i):
        wide = pl.ds(pl.multiple_of(i * group * DN, group * DN), group * DN)
        narrow = pl.ds(pl.multiple_of(i * group * DR, group * DR), group * DR)
        return [
            pltpu.make_async_copy(src.at[:, at], dst.at[:, at], sems.at[i, j])
            for j, (src, dst, at) in enumerate(
                ((wuk, up, wide), (qn, nope, wide), (qr, rotary, narrow))
            )
        ]

    for i in range(steps):
        for copy in copies(i):
            copy.start()

    def ordered(x):
        return jnp.concatenate(
            [
                x[b * half + c * part : b * half + (c + 1) * part]
                for c in range(CHUNKS)
                for b in range(2)
            ],
            0,
        )

    lane = lax.broadcasted_iota(jnp.int32, (rows, KQ - KD), 1)
    ones = jnp.where(lane == 0, 1.0, 0.0).astype(bf16)

    def step(i, _):
        for copy in copies(i):
            copy.wait()
        wide = pl.ds(pl.multiple_of(i * group * DN, group * DN), group * DN)
        narrow = pl.ds(pl.multiple_of(i * group * DR, group * DR), group * DR)
        n, r, w = nope[:, wide], rotary[:, narrow], up[:, wide]
        for g in range(group):
            latent = dot_t(n[:, g * DN : (g + 1) * DN], w[:, g * DN : (g + 1) * DN])
            latent = ordered(latent.astype(bf16))
            rope = ordered(r[:, g * DR : (g + 1) * DR])
            for c in range(CHUNKS):
                q_out[c, i * group + g, :, :KVL] = latent[c * rows : (c + 1) * rows]
                q_out[c, i * group + g, :, KVL:KD] = rope[c * rows : (c + 1) * rows]
                q_out[c, i * group + g, :, KD:] = ones
        return 0

    lax.fori_loop(0, steps, step, 0)


def local_kernel(rels, tokens, group, *refs):
    n = len(rels)
    (limit, q), caches, spans, (acc_out, top_out, sum_out), (kt, k) = split_refs(refs, 2, n, n, 3)
    load_keys(caches, spans, rels, limit[0], tokens, kt, k)
    half = tokens // 2
    part = half // CHUNKS
    rows = tokens // CHUNKS
    steps = q.shape[1] // group
    cached = caches[0].shape[1]
    own = range(cached, cached + tokens)
    row = lax.broadcasted_iota(jnp.int32, (rows, tokens), 0)
    column = lax.broadcasted_iota(jnp.int32, (rows, tokens), 1)

    def place(i):
        return i // steps, slice(i % steps * group, (i % steps + 1) * group)

    def scores(i):
        c, heads = place(i)
        return dot(q[c, heads].reshape(group * rows, KQ), kt[...])

    def finish(i, s):
        c, heads = place(i)
        token = (row // part) * half + c * part + row % part
        later = jnp.where(column > token, MASKED, 0.0)
        here = s[:, own.start : own.stop].reshape(group, rows, tokens) + later[None]
        s = jnp.concatenate(
            [s[:, : own.start], here.reshape(group * rows, tokens), s[:, own.stop :]], 1
        )
        p, total, top = softmax(s, None)
        acc_out[c, heads] = dot(p, k[...]).reshape(group, rows, KVL)
        top_out[c, heads] = top.reshape(group, rows, LANES)
        sum_out[c, heads] = jnp.broadcast_to(total, top.shape).reshape(group, rows, LANES)

    pipelined(CHUNKS * steps, scores, finish)


def rest_kernel(rels, tokens, group, which, *refs):
    n = len(rels)
    (limit, q, acc, top_in, sum_in, wuv), caches, spans, (out,), (kt, k) = split_refs(
        refs, 6, n, n, 1
    )
    load_keys(caches, spans, rels, limit[0], tokens, kt, k)
    rows = tokens // CHUNKS

    def place(i):
        return slice(i * group, (i + 1) * group)

    def scores(i):
        return dot(q[which, place(i)].reshape(group * rows, KQ), kt[...])

    def finish(i, s):
        old = top_in[which, place(i)].reshape(group * rows, LANES)
        p, total, top = softmax(s, old)
        fade = jnp.exp2((old - top) * EXP_SCALE)
        share = 1.0 / (sum_in[which, place(i)].reshape(group * rows, LANES) * fade + total)
        fade = fade * share
        before = lanes(acc[which, place(i)].reshape(group * rows, KVL))
        after = lanes(dot(p, k[...]))
        o = jnp.concatenate(
            [(x * fade + y * share).astype(bf16) for x, y in zip(before, after)], 1
        )
        for g in range(group):
            at = slice((i * group + g) * DV, (i * group + g + 1) * DV)
            out[:, at] = dot(o[g * rows : (g + 1) * rows], wuv[:, at]).astype(bf16)

    pipelined(q.shape[1] // group, scores, finish)


def combinations(bits):
    found = [0]
    for bit in bits:
        found = [x | bit for x in found] + found
    return sorted(found, reverse=True)


def block_order(stages):
    if not stages:
        return [0]
    rest = block_order(stages[1:])
    return [x | r for x in combinations(stages[0]) for r in rest]


def project_kernel(n_tok, per, groups, *refs):
    counts = [len(combinations(stages[0])) for stages, _, _, _ in groups]
    pieces, (w_o,), outs, (lhs,) = split_refs(refs, n_tok, 1, sum(counts))
    part = pieces[0].shape[0] // per
    n = n_tok * per
    me_tok, me_head = lax.axis_index("tok"), lax.axis_index("head")
    for i in range(n_tok):
        for b in range(per):
            rel = ((me_tok ^ i) * per + b) ^ me_head
            start = pl.multiple_of(rel * part, part)
            lhs[pl.ds(start, part), :] = pieces[i][b * part : (b + 1) * part, :]
    for stages, start, count, tile in groups:
        order = block_order(stages)
        ways = len(combinations(stages[0]))
        mine, outs = outs[:ways], outs[ways:]
        rows = n * part // ways
        for t in range(count):
            columns = slice((start + t) * tile, (start + t + 1) * tile)
            here = slice(t * tile, (t + 1) * tile)
            y = dot(lhs[...], w_o[:, columns]).astype(bf16)
            y = jnp.concatenate([y[r * part : (r + 1) * part] for r in order], 0)
            for j, out in enumerate(mine):
                out[:, here] = y[j * rows : (j + 1) * rows]


def shards(q_nope, q_rope, cache_kv, span_kv, w_uk, w_uv, w_o, prefix_length):
    tokens = q_nope.shape[0]
    heads = w_uk.shape[1] // DN
    cache_rows = cache_kv.shape[0]
    n_tok, n_head = lax.axis_size("tok"), lax.axis_size("head")
    per = n_head // n_tok
    rows = tokens // CHUNKS
    params = pltpu.CompilerParams(vmem_limit_bytes=VMEM_LIMIT)
    smem = pl.BlockSpec(memory_space=pltpu.SMEM)
    vmem = pl.BlockSpec(memory_space=pltpu.VMEM)

    def step(held, axis_bit):
        return {rel ^ axis_bit: xor_permute(v, "tok", axis_bit) for rel, v in held.items()}

    def gather(x):
        held = {0: x}
        for bit in reversed(bits_of(n_tok)):
            held.update(step(held, bit))
        return [in_vmem(held[rel]) for rel in range(n_tok)]

    def cost(flops):
        return pl.CostEstimate(flops=flops // COST_SHARE, bytes_accessed=0, transcendentals=0)

    held = {0: (cache_kv.T, span_kv.T)}

    def key_step(held, bit):
        return {
            rel ^ bit: tuple(xor_permute(v, "tok", bit) for v in both)
            for rel, both in held.items()
        }

    for bit in reversed(bits_of(n_tok)[1:]):
        held.update(key_step(held, bit))
    held.update(key_step({0: held[0]}, 1))
    caches = {rel: in_vmem(held[rel][0]) for rel in (0, 1)}
    spans = {rel: in_vmem(held[rel][1]) for rel in (0, 1)}
    near = [rel for rel in range(n_tok) if rel < 2]
    far = [rel for rel in range(n_tok) if rel >= 2]

    def key_scratch(rels):
        keys = len(rels) * (cache_rows + tokens)
        return [
            pltpu.VMEM((KQ, keys), bf16),
            pltpu.VMEM((keys, KVL), bf16),
        ]

    group = math.gcd(heads, 4)
    anywhere = pl.BlockSpec(memory_space=pltpu.HBM)
    q = in_vmem(
        pl.pallas_call(
            functools.partial(query_kernel, tokens, group),
            in_specs=[anywhere] * 3,
            out_specs=vmem,
            out_shape=pltpu.VMEM((CHUNKS, heads, rows, KQ), bf16),
            scratch_shapes=[
                pltpu.VMEM(q_nope.shape, bf16),
                pltpu.VMEM(q_rope.shape, bf16),
                pltpu.VMEM(w_uk.shape, bf16),
                pltpu.SemaphoreType.DMA((heads // group, 3)),
            ],
            compiler_params=params,
            name="query_latent",
            cost_estimate=cost(2 * tokens * w_uk.size),
        )(*[pltpu.with_memory_space_constraint(x, pltpu.HBM) for x in (q_nope, q_rope, w_uk)])
    )
    group = math.gcd(heads, 8)
    state = pl.pallas_call(
        functools.partial(local_kernel, near, tokens, group),
        in_specs=[smem] + [vmem] * (1 + 2 * len(near)),
        out_specs=[vmem] * 3,
        out_shape=[
            pltpu.VMEM((CHUNKS, heads, rows, KVL), f32),
            pltpu.VMEM((CHUNKS, heads, rows, LANES), f32),
            pltpu.VMEM((CHUNKS, heads, rows, LANES), f32),
        ],
        scratch_shapes=key_scratch(near),
        compiler_params=params,
        name="local_keys",
        cost_estimate=cost(4 * tokens * heads * len(near) * (cache_rows + tokens) * KD),
    )(prefix_length, q, *[caches[r] for r in near], *[spans[r] for r in near])
    others = {rel: both for rel, both in held.items() if rel > 1}
    others, state = lax.optimization_barrier((others, state))
    others.update(key_step(others, 1))
    caches.update({rel: in_vmem(both[0]) for rel, both in others.items()})
    spans.update({rel: in_vmem(both[1]) for rel, both in others.items()})
    state = [in_vmem(x) for x in state]

    def rest(which):
        return pl.pallas_call(
            functools.partial(rest_kernel, far, tokens, group, which),
            in_specs=[smem] + [vmem] * (5 + 2 * len(far)),
            out_specs=vmem,
            out_shape=pltpu.VMEM((rows, heads * DV), bf16),
            scratch_shapes=key_scratch(far),
            compiler_params=params,
            name="far_keys",
            cost_estimate=cost(4 * rows * heads * len(far) * (cache_rows + tokens) * KD),
        )(prefix_length, q, *state, in_vmem(w_uv), *[caches[r] for r in far], *[spans[r] for r in far])

    columns = w_o.shape[1]
    depth = w_o.shape[0]
    tile = 256 if columns % 256 == 0 else columns
    tiles = columns // tile
    groups, start = [], 0
    for at, (share, stages) in enumerate(PLAN):
        count = round(tiles * share)
        if at == len(PLAN) - 1:
            count = tiles - start
        if count > 0:
            groups.append((stages(bits_of(n_head)), start, count, tile))
            start += count

    def project(values):
        shapes = [
            pltpu.VMEM((n_head // ways * (rows // per), tile * count), bf16)
            for ways, count in (
                (len(combinations(stages[0])), count) for stages, _, count, _ in groups
            )
            for _ in range(ways)
        ]
        return pl.pallas_call(
            functools.partial(project_kernel, n_tok, per, groups),
            in_specs=[vmem] * (n_tok + 1),
            out_specs=[vmem] * len(shapes),
            out_shape=shapes,
            scratch_shapes=[pltpu.VMEM((n_head // per * rows, depth), bf16)],
            compiler_params=params,
            name="project",
            cost_estimate=cost(2 * n_head // per * rows * depth * columns),
        )(*values, in_vmem(w_o))

    def scatter(parts, stages):
        for at, bits in enumerate(stages):
            moves = combinations(bits)[:-1]
            got = [xor_permute(x, "head", move) for x, move in zip(parts, moves)]
            terms = [parts[-1]] + got
            ways = len(combinations(stages[at + 1])) if at + 1 < len(stages) else 1
            size = terms[0].shape[0] // ways
            parts = [
                sum(x[j * size : (j + 1) * size].astype(f32) for x in terms).astype(bf16)
                for j in range(ways)
            ]
        return parts[0]

    out = []
    for which in range(CHUNKS):
        parts = list(project(gather(rest(which))))
        ends = []
        for stages, _, _, _ in groups:
            ways = len(combinations(stages[0]))
            ends.append(scatter(parts[:ways], stages))
            parts = parts[ways:]
        out.append(jnp.concatenate(ends, 1))
    return jnp.concatenate(out, 0)


def solution(mesh):
    return jax.shard_map(
        shards,
        mesh=mesh,
        in_specs=(
            P("tok", "head"),
            P("tok", "head"),
            P("tok", None),
            P("tok", None),
            P(None, "head"),
            P(None, "head"),
            P("head", "tok"),
            P(),
        ),
        out_specs=P("head", "tok"),
        check_vma=False,
    )
```

time: 73 us -> 64.9 us (0.89)
  Pallas kernels: 20.2 us -> 14.7 us
  starting transfers between devices: 26.1 us -> 22.2 us
  waiting for transfers between devices: 24.6 us -> 25.8 us
    pallas_call x2, Pallas kernels: 9.05 us -> 4.85 us  [rest(): pl.pallas_call(functools.partial(rest_kernel, far, tokens, group, which),...]
    ppermute x24, starting transfers between devices: 26.1 us -> 22.2 us  [xor_permute(): return lax.ppermute(x, axis, [(i, i ^ bit) for i in range(n)])]
    ppermute x24, waiting for transfers between devices: 24.6 us -> 25.8 us  [xor_permute(): return lax.ppermute(x, axis, [(i, i ^ bit) for i in range(n)])]
    pallas_call x1, Pallas kernels: 4.12 us -> 3.04 us  [shards(): pl.pallas_call(functools.partial(local_kernel, near, tokens, group), in_s...]
  transfers between devices with their start and end apart: 24 -> 24, of which waited for: 11 -> 12; matrix products, arithmetic and copies ran while one was open for 1% -> 1% of each run, Pallas kernels for 21% -> 19%
where the time goes in v2:
time: 64.9 us; the launch traced here: 64.8 us
  waiting for transfers between devices  25.8 us (40%)
  starting transfers between devices  22.2 us (34%)
  Pallas kernels  14.7 us (23%)
  other arithmetic  1.1 us (2%)
  between operations  0.87 us (1%)
    ppermute x24, waiting for transfers between devices, xor_permute(): return lax.ppermute(x, axis, [(i, i ^ bit) for i in range(n)])  25.8 us
    ppermute x24, starting transfers between devices, xor_permute(): return lax.ppermute(x, axis, [(i, i ^ bit) for i in range(n)])  22.2 us
    pallas_call x2, Pallas kernels, rest(): pl.pallas_call(functools.partial(rest_kernel, far, tokens, group, which),...  4.85 us
    pallas_call x2, Pallas kernels, project(): pl.pallas_call(functools.partial(project_kernel, n_tok, per, groups), in_...  4.23 us
    pallas_call x1, Pallas kernels, shards(): pl.pallas_call(functools.partial(local_kernel, near, tokens, group), in_s...  3.04 us
    pallas_call x1, Pallas kernels, shards(): pl.pallas_call(functools.partial(query_kernel, tokens, group), in_specs=[...  2.59 us
  transfers between devices with their start and end apart: 24, of which 12 were waited for; matrix products, arithmetic and copies ran while one was open for 1% of the time, Pallas kernels for 19%

profile of v2, /device:TPU:0, one launch (start us, length us, event | category | flops | bytes accessed | tf_op | source)
XLA Modules:
  0.0 64.8 jit_solution(810499267520580276)
XLA Ops:
  0.5 2.9 %collective-permute-start = (bf16[576,128]{1,0:T(8,128)(2,1)}, bf16[576,128]{1,0:T(8,128)(2,1)S(1)}, u32[]{:S(2)}, u32[]{:S(2)}) collective-permute-start(bf16[576,128]{1,0:T(8,128)(2,1)} %bitcast.5), channel_id=1, source_target_pairs={{0,16},{8,24},{16,0},{24,8},{1,17},{9,25},{17,1},{25,9},{2,18},{10... | collective-permute-start | bytes 442376 | tf_op jit(solution)/shard_map/ppermute | solution.py:43
  4.2 2.6 %query_latent.1.refs_1_ = bf16[2,16,64,640]{3,2,1,0:T(8,128)(2,1)S(1)} custom-call(bf16[128,2048]{1,0:T(8,128)(2,1)} %qn.1, bf16[128,1024]{1,0:T(8,128)(2,1)} %qr.1, bf16[512,2048]{1,0:T(8,128)(2,1)} %wuk.1), custom_call_target="tpu_custom_call" | custom-call | flops 268435456 | tf_op jit(solution)/shard_map/query_latent/pallas_call | solution.py:314
  6.8 3.0 %local_keys.1 = (f32[2,16,64,512]{3,2,1,0:T(8,128)S(1)}, f32[2,16,64,128]{3,2,1,0:T(8,128)S(1)}, f32[2,16,64,128]{3,2,1,0:T(8,128)S(1)}) custom-call(s32[1]{0:T(128)S(6)} %copy.9.refs_0_, bf16[2,16,64,640]{3,2,1,0:T(8,128)(2,1)S(1)} %query_latent.1.refs_1_, bf16[576,128]{1,0:T(8,128)(2,1)S(1)} %bitcast.6, ...), custom_call_target="tpu_custom_call" | custom-call | flops 2415919104 | tf_op jit(solution)/shard_map/local_keys/pallas_call | solution.py:331
  12.4 2.4 %far_keys.2.refs_0_ = bf16[64,2048]{1,0:T(8,128)(2,1)S(1)} custom-call(s32[1]{0:T(128)S(6)} %copy.9.refs_0_, bf16[2,16,64,640]{3,2,1,0:T(8,128)(2,1)S(1)} %query_latent.1.refs_1_, f32[2,16,64,512]{3,2,1,0:T(8,128)S(1)} %get-tuple-element.24.refs_2_, f32[2,16,64,128]{3,2,1,0:T(8,128)S(1)} %get-tuple-element.25.refs_3_, ...), custom_call_target="tpu_custom_call" | custom-call | flops 1207959552 | tf_op jit(solution)/shard_map/far_keys/pallas_call | solution.py:353
  14.9 1.8 %collective-permute-start.7 = (bf16[64,2048]{1,0:T(8,128)(2,1)S(1)}, bf16[64,2048]{1,0:T(8,128)(2,1)S(1)}, u32[]{:S(2)}, u32[]{:S(2)}) collective-permute-start(bf16[64,2048]{1,0:T(8,128)(2,1)S(1)} %far_keys.2.refs_0_), channel_id=1, source_target_pairs={{0,16},{8,24},{16,0},{24,8},{1,17},{9,25},{17,1},{25,9},{2,18},{10... | collective-permute-start | bytes 786440 | tf_op jit(solution)/shard_map/ppermute | solution.py:43
  16.7 2.4 %far_keys.3.refs_0_ = bf16[64,2048]{1,0:T(8,128)(2,1)S(1)} custom-call(s32[1]{0:T(128)S(6)} %copy.9.refs_0_, bf16[2,16,64,640]{3,2,1,0:T(8,128)(2,1)S(1)} %query_latent.1.refs_1_, f32[2,16,64,512]{3,2,1,0:T(8,128)S(1)} %get-tuple-element.24.refs_2_, f32[2,16,64,128]{3,2,1,0:T(8,128)S(1)} %get-tuple-element.25.refs_3_, ...), custom_call_target="tpu_custom_call" | custom-call | flops 1207959552 | tf_op jit(solution)/shard_map/far_keys/pallas_call | solution.py:353
  19.4 4.6 %collective-permute-done.7.refs_2_ = bf16[64,2048]{1,0:T(8,128)(2,1)S(1)} collective-permute-done((bf16[64,2048]{1,0:T(8,128)(2,1)S(1)}, bf16[64,2048]{1,0:T(8,128)(2,1)S(1)}, u32[]{:S(2)}, u32[]{:S(2)}) %collective-permute-start.7) | collective-permute-done | bytes 262176 | tf_op jit(solution)/shard_map/ppermute | solution.py:43
  24.6 4.5 %collective-permute-done.16.refs_2_ = bf16[64,2048]{1,0:T(8,128)(2,1)S(1)} collective-permute-done((bf16[64,2048]{1,0:T(8,128)(2,1)S(1)}, bf16[64,2048]{1,0:T(8,128)(2,1)S(1)}, u32[]{:S(2)}, u32[]{:S(2)}) %collective-permute-start.16) | collective-permute-done | bytes 262176 | tf_op jit(solution)/shard_map/ppermute | solution.py:43
  29.1 2.1 %project.2 = (bf16[128,1024]{1,0:T(8,128)(2,1)S(1)}, bf16[128,1024]{1,0:T(8,128)(2,1)S(1)}, bf16[128,768]{1,0:T(8,128)(2,1)S(1)}, bf16[128,768]{1,0:T(8,128)(2,1)S(1)}) custom-call(bf16[64,2048]{1,0:T(8,128)(2,1)S(1)} %far_keys.2.refs_0_, bf16[64,2048]{1,0:T(8,128)(2,1)S(1)} %collective-permute-done.6.refs_1_, ...), custom_call_target="tpu_custom_call" | custom-call | flops 1879048192 | tf_op jit(solution)/shard_map/project/pallas_call | solution.py:385
  31.2 1.9 %collective-permute-start.12 = (bf16[128,768]{1,0:T(8,128)(2,1)S(1)}, bf16[128,768]{1,0:T(8,128)(2,1)S(1)}, u32[]{:S(2)}, u32[]{:S(2)}) collective-permute-start(bf16[128,768]{1,0:T(8,128)(2,1)S(1)} %get-tuple-element.32), channel_id=1, source_target_pairs={{0,2},{1,3},{2,0},{3,1},{4,6},{5,7},{6,4},{7,5},{8,10},{9,11},{10,... | collective-permute-start | bytes 589832 | tf_op jit(solution)/shard_map/ppermute | solution.py:43
  33.1 1.5 %collective-permute-start.9 = (bf16[128,1024]{1,0:T(8,128)(2,1)S(1)}, bf16[128,1024]{1,0:T(8,128)(2,1)S(1)}, u32[]{:S(2)}, u32[]{:S(2)}) collective-permute-start(bf16[128,1024]{1,0:T(8,128)(2,1)S(1)} %get-tuple-element.30), channel_id=1, source_target_pairs={{0,1},{1,0},{2,3},{3,2},{4,5},{5,4},{6,7},{7,6},{8,9},{9,8},{10,11... | collective-permute-start | bytes 786440 | tf_op jit(solution)/shard_map/ppermute | solution.py:43
  34.6 2.1 %project.3 = (bf16[128,1024]{1,0:T(8,128)(2,1)S(1)}, bf16[128,1024]{1,0:T(8,128)(2,1)S(1)}, bf16[128,768]{1,0:T(8,128)(2,1)S(1)}, bf16[128,768]{1,0:T(8,128)(2,1)S(1)}) custom-call(bf16[64,2048]{1,0:T(8,128)(2,1)S(1)} %far_keys.3.refs_0_, bf16[64,2048]{1,0:T(8,128)(2,1)S(1)} %collective-permute-done.15.refs_1_, ...), custom_call_target="tpu_custom_call" | custom-call | flops 1879048192 | tf_op jit(solution)/shard_map/project/pallas_call | solution.py:385
  37.6 1.1 %collective-permute-done.12 = bf16[128,768]{1,0:T(8,128)(2,1)S(1)} collective-permute-done((bf16[128,768]{1,0:T(8,128)(2,1)S(1)}, bf16[128,768]{1,0:T(8,128)(2,1)S(1)}, u32[]{:S(2)}, u32[]{:S(2)}) %collective-permute-start.12) | collective-permute-done | bytes 196640 | tf_op jit(solution)/shard_map/ppermute | solution.py:43
  38.7 2.8 %collective-permute-start.13 = (bf16[64,768]{1,0:T(8,128)(2,1)S(1)}, bf16[64,768]{1,0:T(8,128)(2,1)S(1)}, u32[]{:S(2)}, u32[]{:S(2)}) collective-permute-start(bf16[64,768]{1,0:T(8,128)(2,1)S(1)} %get-tuple-element.42), channel_id=1, source_target_pairs={{0,4},{1,5},{2,6},{3,7},{4,0},{5,1},{6,2},{7,3},{8,12},{9,13},{10,... | collective-permute-start | bytes 294920 | tf_op jit(solution)/shard_map/ppermute | solution.py:43
  41.5 4.1 %collective-permute-done.21 = bf16[128,768]{1,0:T(8,128)(2,1)S(1)} collective-permute-done((bf16[128,768]{1,0:T(8,128)(2,1)S(1)}, bf16[128,768]{1,0:T(8,128)(2,1)S(1)}, u32[]{:S(2)}, u32[]{:S(2)}) %collective-permute-start.21) | collective-permute-done | bytes 196640 | tf_op jit(solution)/shard_map/ppermute | solution.py:43
  45.7 1.6 %collective-permute-start.22 = (bf16[64,768]{1,0:T(8,128)(2,1)S(1)}, bf16[64,768]{1,0:T(8,128)(2,1)S(1)}, u32[]{:S(2)}, u32[]{:S(2)}) collective-permute-start(bf16[64,768]{1,0:T(8,128)(2,1)S(1)} %get-tuple-element.44), channel_id=1, source_target_pairs={{0,4},{1,5},{2,6},{3,7},{4,0},{5,1},{6,2},{7,3},{8,12},{9,13},{10,... | collective-permute-start | bytes 294920 | tf_op jit(solution)/shard_map/ppermute | solution.py:43
  48.3 1.3 %collective-permute-start.19 = (bf16[64,1024]{1,0:T(8,128)(2,1)S(1)}, bf16[64,1024]{1,0:T(8,128)(2,1)S(1)}, u32[]{:S(2)}, u32[]{:S(2)}) collective-permute-start(bf16[64,1024]{1,0:T(8,128)(2,1)S(1)} %get-tuple-element.40), channel_id=1, source_target_pairs={{0,2},{1,3},{2,0},{3,1},{4,6},{5,7},{6,4},{7,5},{8,10},{9,11},{10,... | collective-permute-start | bytes 393224 | tf_op jit(solution)/shard_map/ppermute | solution.py:43
  50.3 1.8 %collective-permute-done.22 = bf16[64,768]{1,0:T(8,128)(2,1)S(1)} collective-permute-done((bf16[64,768]{1,0:T(8,128)(2,1)S(1)}, bf16[64,768]{1,0:T(8,128)(2,1)S(1)}, u32[]{:S(2)}, u32[]{:S(2)}) %collective-permute-start.22) | collective-permute-done | bytes 98336 | tf_op jit(solution)/shard_map/ppermute | solution.py:43
  52.1 1.1 %collective-permute-start.23 = (bf16[32,768]{1,0:T(8,128)(2,1)S(1)}, bf16[32,768]{1,0:T(8,128)(2,1)S(1)}, u32[]{:S(2)}, u32[]{:S(2)}) collective-permute-start(bf16[32,768]{1,0:T(8,128)(2,1)S(1)} %add_convert_fusion.15), channel_id=1, source_target_pairs={{0,1},{1,0},{2,3},{3,2},{4,5},{5,4},{6,7},{7,6},{8,9},{9,8},{10,11... | collective-permute-start | bytes 147464 | tf_op jit(solution)/shard_map/ppermute | solution.py:43
  53.8 2.4 %collective-permute-done.23 = bf16[32,768]{1,0:T(8,128)(2,1)S(1)} collective-permute-done((bf16[32,768]{1,0:T(8,128)(2,1)S(1)}, bf16[32,768]{1,0:T(8,128)(2,1)S(1)}, u32[]{:S(2)}, u32[]{:S(2)}) %collective-permute-start.23) | collective-permute-done | bytes 49184 | tf_op jit(solution)/shard_map/ppermute | solution.py:43
  56.3 1.9 %collective-permute-start.11 = (bf16[32,1024]{1,0:T(8,128)(2,1)S(1)}, bf16[32,1024]{1,0:T(8,128)(2,1)S(1)}, u32[]{:S(2)}, u32[]{:S(2)}) collective-permute-start(bf16[32,1024]{1,0:T(8,128)(2,1)S(1)} %add_convert_fusion.12), channel_id=1, source_target_pairs={{0,4},{1,5},{2,6},{3,7},{4,0},{5,1},{6,2},{7,3},{8,12},{9,13},{10,... | collective-permute-start | bytes 196616 | tf_op jit(solution)/shard_map/ppermute | solution.py:43
  58.2 1.2 %collective-permute-start.20 = (bf16[32,1024]{1,0:T(8,128)(2,1)S(1)}, bf16[32,1024]{1,0:T(8,128)(2,1)S(1)}, u32[]{:S(2)}, u32[]{:S(2)}) collective-permute-start(bf16[32,1024]{1,0:T(8,128)(2,1)S(1)} %add_convert_fusion.9), channel_id=1, source_target_pairs={{0,4},{1,5},{2,6},{3,7},{4,0},{5,1},{6,2},{7,3},{8,12},{9,13},{10,... | collective-permute-start | bytes 196616 | tf_op jit(solution)/shard_map/ppermute | solution.py:43
  59.4 2.6 %collective-permute-done.11 = bf16[32,1024]{1,0:T(8,128)(2,1)S(1)} collective-permute-done((bf16[32,1024]{1,0:T(8,128)(2,1)S(1)}, bf16[32,1024]{1,0:T(8,128)(2,1)S(1)}, u32[]{:S(2)}, u32[]{:S(2)}) %collective-permute-start.11) | collective-permute-done | bytes 65568 | tf_op jit(solution)/shard_map/ppermute | solution.py:43
  62.0 2.0 %collective-permute-done.20 = bf16[32,1024]{1,0:T(8,128)(2,1)S(1)} collective-permute-done((bf16[32,1024]{1,0:T(8,128)(2,1)S(1)}, bf16[32,1024]{1,0:T(8,128)(2,1)S(1)}, u32[]{:S(2)}, u32[]{:S(2)}) %collective-permute-start.20) | collective-permute-done | bytes 65568 | tf_op jit(solution)/shard_map/ppermute | solution.py:43
  (54 shorter events, 8.0 us)
Async XLA Ops:
  0.0 6.8 %collective-permute-start.2 = (bf16[576,128]{1,0:T(8,128)(2,1)}, bf16[576,128]{1,0:T(8,128)(2,1)S(1)}, u32[]{:S(2)}, u32[]{:S(2)}) collective-permute-start(bf16[576,128]{1,0:T(8,128)(2,1)} %bitcast.4), channel_id=1, source_target_pairs={{0,8},{8,0},{16,24},{24,16},{1,9},{9,1},{17,25},{25,17},{2,10},{10... | collective-permute-start | bytes 442376 | tf_op jit(solution)/shard_map/ppermute | solution.py:43
  0.5 6.3 %collective-permute-start.3 = (bf16[576,128]{1,0:T(8,128)(2,1)}, bf16[576,128]{1,0:T(8,128)(2,1)S(1)}, u32[]{:S(2)}, u32[]{:S(2)}) collective-permute-start(bf16[576,128]{1,0:T(8,128)(2,1)} %bitcast.7), channel_id=1, source_target_pairs={{0,8},{8,0},{16,24},{24,16},{1,9},{9,1},{17,25},{25,17},{2,10},{10... | collective-permute-start | bytes 442376 | tf_op jit(solution)/shard_map/ppermute | solution.py:43
  0.5 9.3 %collective-permute-start = (bf16[576,128]{1,0:T(8,128)(2,1)}, bf16[576,128]{1,0:T(8,128)(2,1)S(1)}, u32[]{:S(2)}, u32[]{:S(2)}) collective-permute-start(bf16[576,128]{1,0:T(8,128)(2,1)} %bitcast.5), channel_id=1, source_target_pairs={{0,16},{8,24},{16,0},{24,8},{1,17},{9,25},{17,1},{25,9},{2,18},{10... | collective-permute-start | bytes 442376 | tf_op jit(solution)/shard_map/ppermute | solution.py:43
  3.5 7.4 %collective-permute-start.1 = (bf16[576,128]{1,0:T(8,128)(2,1)}, bf16[576,128]{1,0:T(8,128)(2,1)S(1)}, u32[]{:S(2)}, u32[]{:S(2)}) collective-permute-start(bf16[576,128]{1,0:T(8,128)(2,1)} %bitcast.8), channel_id=1, source_target_pairs={{0,16},{8,24},{16,0},{24,8},{1,17},{9,25},{17,1},{25,9},{2,18},{10... | collective-permute-start | bytes 442376 | tf_op jit(solution)/shard_map/ppermute | solution.py:43
  10.8 1.4 %collective-permute-start.4 = (bf16[576,128]{1,0:T(8,128)(2,1)S(1)}, bf16[576,128]{1,0:T(8,128)(2,1)S(1)}, u32[]{:S(2)}, u32[]{:S(2)}) collective-permute-start(bf16[576,128]{1,0:T(8,128)(2,1)S(1)} %collective-permute-done.refs_6_), channel_id=1, source_target_pairs={{0,8},{8,0},{16,24},{24,16},{1,9},{9,1},{17,25},{25,17},{2,10},{10... | collective-permute-start | bytes 442376 | tf_op jit(solution)/shard_map/ppermute | solution.py:43
  10.8 1.6 %collective-permute-start.5 = (bf16[576,128]{1,0:T(8,128)(2,1)S(1)}, bf16[576,128]{1,0:T(8,128)(2,1)S(1)}, u32[]{:S(2)}, u32[]{:S(2)}) collective-permute-start(bf16[576,128]{1,0:T(8,128)(2,1)S(1)} %collective-permute-done.1.refs_8_), channel_id=1, source_target_pairs={{0,8},{8,0},{16,24},{24,16},{1,9},{9,1},{17,25},{25,17},{2,10},{10... | collective-permute-start | bytes 442376 | tf_op jit(solution)/shard_map/ppermute | solution.py:43
  14.9 9.2 %collective-permute-start.7 = (bf16[64,2048]{1,0:T(8,128)(2,1)S(1)}, bf16[64,2048]{1,0:T(8,128)(2,1)S(1)}, u32[]{:S(2)}, u32[]{:S(2)}) collective-permute-start(bf16[64,2048]{1,0:T(8,128)(2,1)S(1)} %far_keys.2.refs_0_), channel_id=1, source_target_pairs={{0,16},{8,24},{16,0},{24,8},{1,17},{9,25},{17,1},{25,9},{2,18},{10... | collective-permute-start | bytes 786440 | tf_op jit(solution)/shard_map/ppermute | solution.py:43
  19.1 10.0 %collective-permute-start.16 = (bf16[64,2048]{1,0:T(8,128)(2,1)S(1)}, bf16[64,2048]{1,0:T(8,128)(2,1)S(1)}, u32[]{:S(2)}, u32[]{:S(2)}) collective-permute-start(bf16[64,2048]{1,0:T(8,128)(2,1)S(1)} %far_keys.3.refs_0_), channel_id=1, source_target_pairs={{0,16},{8,24},{16,0},{24,8},{1,17},{9,25},{17,1},{25,9},{2,18},{10... | collective-permute-start | bytes 786440 | tf_op jit(solution)/shard_map/ppermute | solution.py:43
  19.4 9.6 %collective-permute-start.6 = (bf16[64,2048]{1,0:T(8,128)(2,1)S(1)}, bf16[64,2048]{1,0:T(8,128)(2,1)S(1)}, u32[]{:S(2)}, u32[]{:S(2)}) collective-permute-start(bf16[64,2048]{1,0:T(8,128)(2,1)S(1)} %far_keys.2.refs_0_), channel_id=1, source_target_pairs={{0,8},{8,0},{16,24},{24,16},{1,9},{9,1},{17,25},{25,17},{2,10},{10... | collective-permute-start | bytes 786440 | tf_op jit(solution)/shard_map/ppermute | solution.py:43
  24.1 5.0 %collective-permute-start.8 = (bf16[64,2048]{1,0:T(8,128)(2,1)S(1)}, bf16[64,2048]{1,0:T(8,128)(2,1)S(1)}, u32[]{:S(2)}, u32[]{:S(2)}) collective-permute-start(bf16[64,2048]{1,0:T(8,128)(2,1)S(1)} %collective-permute-done.7.refs_2_), channel_id=1, source_target_pairs={{0,8},{8,0},{16,24},{24,16},{1,9},{9,1},{17,25},{25,17},{2,10},{10... | collective-permute-start | bytes 786440 | tf_op jit(solution)/shard_map/ppermute | solution.py:43
  24.1 10.6 %collective-permute-start.15 = (bf16[64,2048]{1,0:T(8,128)(2,1)S(1)}, bf16[64,2048]{1,0:T(8,128)(2,1)S(1)}, u32[]{:S(2)}, u32[]{:S(2)}) collective-permute-start(bf16[64,2048]{1,0:T(8,128)(2,1)S(1)} %far_keys.3.refs_0_), channel_id=1, source_target_pairs={{0,8},{8,0},{16,24},{24,16},{1,9},{9,1},{17,25},{25,17},{2,10},{10... | collective-permute-start | bytes 786440 | tf_op jit(solution)/shard_map/ppermute | solution.py:43
  29.1 5.6 %collective-permute-start.17 = (bf16[64,2048]{1,0:T(8,128)(2,1)S(1)}, bf16[64,2048]{1,0:T(8,128)(2,1)S(1)}, u32[]{:S(2)}, u32[]{:S(2)}) collective-permute-start(bf16[64,2048]{1,0:T(8,128)(2,1)S(1)} %collective-permute-done.16.refs_2_), channel_id=1, source_target_pairs={{0,8},{8,0},{16,24},{24,16},{1,9},{9,1},{17,25},{25,17},{2,10},{10... | collective-permute-start | bytes 786440 | tf_op jit(solution)/shard_map/ppermute | solution.py:43
  31.2 7.5 %collective-permute-start.12 = (bf16[128,768]{1,0:T(8,128)(2,1)S(1)}, bf16[128,768]{1,0:T(8,128)(2,1)S(1)}, u32[]{:S(2)}, u32[]{:S(2)}) collective-permute-start(bf16[128,768]{1,0:T(8,128)(2,1)S(1)} %get-tuple-element.32), channel_id=1, source_target_pairs={{0,2},{1,3},{2,0},{3,1},{4,6},{5,7},{6,4},{7,5},{8,10},{9,11},{10,... | collective-permute-start | bytes 589832 | tf_op jit(solution)/shard_map/ppermute | solution.py:43
  33.1 14.2 %collective-permute-start.9 = (bf16[128,1024]{1,0:T(8,128)(2,1)S(1)}, bf16[128,1024]{1,0:T(8,128)(2,1)S(1)}, u32[]{:S(2)}, u32[]{:S(2)}) collective-permute-start(bf16[128,1024]{1,0:T(8,128)(2,1)S(1)} %get-tuple-element.30), channel_id=1, source_target_pairs={{0,1},{1,0},{2,3},{3,2},{4,5},{5,4},{6,7},{7,6},{8,9},{9,8},{10,11... | collective-permute-start | bytes 786440 | tf_op jit(solution)/shard_map/ppermute | solution.py:43
  36.8 8.9 %collective-permute-start.21 = (bf16[128,768]{1,0:T(8,128)(2,1)S(1)}, bf16[128,768]{1,0:T(8,128)(2,1)S(1)}, u32[]{:S(2)}, u32[]{:S(2)}) collective-permute-start(bf16[128,768]{1,0:T(8,128)(2,1)S(1)} %get-tuple-element.36), channel_id=1, source_target_pairs={{0,2},{1,3},{2,0},{3,1},{4,6},{5,7},{6,4},{7,5},{8,10},{9,11},{10,... | collective-permute-start | bytes 589832 | tf_op jit(solution)/shard_map/ppermute | solution.py:43
  37.3 11.0 %collective-permute-start.18 = (bf16[128,1024]{1,0:T(8,128)(2,1)S(1)}, bf16[128,1024]{1,0:T(8,128)(2,1)S(1)}, u32[]{:S(2)}, u32[]{:S(2)}) collective-permute-start(bf16[128,1024]{1,0:T(8,128)(2,1)S(1)} %get-tuple-element.34), channel_id=1, source_target_pairs={{0,1},{1,0},{2,3},{3,2},{4,5},{5,4},{6,7},{7,6},{8,9},{9,8},{10,11... | collective-permute-start | bytes 786440 | tf_op jit(solution)/shard_map/ppermute | solution.py:43
  38.7 10.9 %collective-permute-start.13 = (bf16[64,768]{1,0:T(8,128)(2,1)S(1)}, bf16[64,768]{1,0:T(8,128)(2,1)S(1)}, u32[]{:S(2)}, u32[]{:S(2)}) collective-permute-start(bf16[64,768]{1,0:T(8,128)(2,1)S(1)} %get-tuple-element.42), channel_id=1, source_target_pairs={{0,4},{1,5},{2,6},{3,7},{4,0},{5,1},{6,2},{7,3},{8,12},{9,13},{10,... | collective-permute-start | bytes 294920 | tf_op jit(solution)/shard_map/ppermute | solution.py:43
  45.7 6.3 %collective-permute-start.22 = (bf16[64,768]{1,0:T(8,128)(2,1)S(1)}, bf16[64,768]{1,0:T(8,128)(2,1)S(1)}, u32[]{:S(2)}, u32[]{:S(2)}) collective-permute-start(bf16[64,768]{1,0:T(8,128)(2,1)S(1)} %get-tuple-element.44), channel_id=1, source_target_pairs={{0,4},{1,5},{2,6},{3,7},{4,0},{5,1},{6,2},{7,3},{8,12},{9,13},{10,... | collective-permute-start | bytes 294920 | tf_op jit(solution)/shard_map/ppermute | solution.py:43
  47.4 8.9 %collective-permute-start.10 = (bf16[64,1024]{1,0:T(8,128)(2,1)S(1)}, bf16[64,1024]{1,0:T(8,128)(2,1)S(1)}, u32[]{:S(2)}, u32[]{:S(2)}) collective-permute-start(bf16[64,1024]{1,0:T(8,128)(2,1)S(1)} %get-tuple-element.38), channel_id=1, source_target_pairs={{0,2},{1,3},{2,0},{3,1},{4,6},{5,7},{6,4},{7,5},{8,10},{9,11},{10,... | collective-permute-start | bytes 393224 | tf_op jit(solution)/shard_map/ppermute | solution.py:43
  48.3 9.9 %collective-permute-start.19 = (bf16[64,1024]{1,0:T(8,128)(2,1)S(1)}, bf16[64,1024]{1,0:T(8,128)(2,1)S(1)}, u32[]{:S(2)}, u32[]{:S(2)}) collective-permute-start(bf16[64,1024]{1,0:T(8,128)(2,1)S(1)} %get-tuple-element.40), channel_id=1, source_target_pairs={{0,2},{1,3},{2,0},{3,1},{4,6},{5,7},{6,4},{7,5},{8,10},{9,11},{10,... | collective-permute-start | bytes 393224 | tf_op jit(solution)/shard_map/ppermute | solution.py:43
  49.6 4.2 %collective-permute-start.14 = (bf16[32,768]{1,0:T(8,128)(2,1)S(1)}, bf16[32,768]{1,0:T(8,128)(2,1)S(1)}, u32[]{:S(2)}, u32[]{:S(2)}) collective-permute-start(bf16[32,768]{1,0:T(8,128)(2,1)S(1)} %add_convert_fusion.18), channel_id=1, source_target_pairs={{0,1},{1,0},{2,3},{3,2},{4,5},{5,4},{6,7},{7,6},{8,9},{9,8},{10,11... | collective-permute-start | bytes 147464 | tf_op jit(solution)/shard_map/ppermute | solution.py:43
  52.1 4.2 %collective-permute-start.23 = (bf16[32,768]{1,0:T(8,128)(2,1)S(1)}, bf16[32,768]{1,0:T(8,128)(2,1)S(1)}, u32[]{:S(2)}, u32[]{:S(2)}) collective-permute-start(bf16[32,768]{1,0:T(8,128)(2,1)S(1)} %add_convert_fusion.15), channel_id=1, source_target_pairs={{0,1},{1,0},{2,3},{3,2},{4,5},{5,4},{6,7},{7,6},{8,9},{9,8},{10,11... | collective-permute-start | bytes 147464 | tf_op jit(solution)/shard_map/ppermute | solution.py:43
  56.3 5.7 %collective-permute-start.11 = (bf16[32,1024]{1,0:T(8,128)(2,1)S(1)}, bf16[32,1024]{1,0:T(8,128)(2,1)S(1)}, u32[]{:S(2)}, u32[]{:S(2)}) collective-permute-start(bf16[32,1024]{1,0:T(8,128)(2,1)S(1)} %add_convert_fusion.12), channel_id=1, source_target_pairs={{0,4},{1,5},{2,6},{3,7},{4,0},{5,1},{6,2},{7,3},{8,12},{9,13},{10,... | collective-permute-start | bytes 196616 | tf_op jit(solution)/shard_map/ppermute | solution.py:43
  58.2 5.8 %collective-permute-start.20 = (bf16[32,1024]{1,0:T(8,128)(2,1)S(1)}, bf16[32,1024]{1,0:T(8,128)(2,1)S(1)}, u32[]{:S(2)}, u32[]{:S(2)}) collective-permute-start(bf16[32,1024]{1,0:T(8,128)(2,1)S(1)} %add_convert_fusion.9), channel_id=1, source_target_pairs={{0,4},{1,5},{2,6},{3,7},{4,0},{5,1},{6,2},{7,3},{8,12},{9,13},{10,... | collective-permute-start | bytes 196616 | tf_op jit(solution)/shard_map/ppermute | solution.py:43
  (5 other events, 41.9 us)

commit v3 on v2

--- a/solution.py
+++ b/solution.py
@@ -23,6 +23,7 @@
     (0.43, lambda bits: [(b,) for b in bits[1:] + bits[:1]]),
 )
 COST_SHARE = 1
+AHEAD = 1
 VMEM_LIMIT = 24 * 1024 * 1024
 EXP_SCALE = math.log2(math.e) / math.sqrt(DN + DR)
 
@@ -191,13 +192,14 @@
     pipelined(CHUNKS * steps, scores, finish)
 
 
-def rest_kernel(rels, tokens, group, which, *refs):
+def step_kernel(rels, tokens, group, which, last, *refs):
     n = len(rels)
-    (limit, q, acc, top_in, sum_in, wuv), caches, spans, (out,), (kt, k) = split_refs(
-        refs, 6, n, n, 1
+    (limit, q, acc, top_in, sum_in, *up), caches, spans, outs, (kt, k) = split_refs(
+        refs, 6 if last else 5, n, n, 1 if last else 3
     )
     load_keys(caches, spans, rels, limit[0], tokens, kt, k)
     rows = tokens // CHUNKS
+    at_state = which if acc.shape[0] == CHUNKS else 0
 
     def place(i):
         return slice(i * group, (i + 1) * group)
@@ -206,19 +208,27 @@
         return dot(q[which, place(i)].reshape(group * rows, KQ), kt[...])
 
     def finish(i, s):
-        old = top_in[which, place(i)].reshape(group * rows, LANES)
+        old = top_in[at_state, place(i)].reshape(group * rows, LANES)
         p, total, top = softmax(s, old)
         fade = jnp.exp2((old - top) * EXP_SCALE)
-        share = 1.0 / (sum_in[which, place(i)].reshape(group * rows, LANES) * fade + total)
+        total = sum_in[at_state, place(i)].reshape(group * rows, LANES) * fade + total
+        before = lanes(acc[at_state, place(i)].reshape(group * rows, KVL))
+        after = lanes(dot(p, k[...]))
+        if not last:
+            acc_out, top_out, sum_out = outs
+            o = jnp.concatenate([x * fade + y for x, y in zip(before, after)], 1)
+            acc_out[0, place(i)] = o.reshape(group, rows, KVL)
+            top_out[0, place(i)] = top.reshape(group, rows, LANES)
+            sum_out[0, place(i)] = total.reshape(group, rows, LANES)
+            return
+        share = 1.0 / total
         fade = fade * share
-        before = lanes(acc[which, place(i)].reshape(group * rows, KVL))
-        after = lanes(dot(p, k[...]))
         o = jnp.concatenate(
             [(x * fade + y * share).astype(bf16) for x, y in zip(before, after)], 1
         )
         for g in range(group):
             at = slice((i * group + g) * DV, (i * group + g + 1) * DV)
-            out[:, at] = dot(o[g * rows : (g + 1) * rows], wuv[:, at]).astype(bf16)
+            outs[0][:, at] = dot(o[g * rows : (g + 1) * rows], up[0][:, at]).astype(bf16)
 
     pipelined(q.shape[1] // group, scores, finish)
 
@@ -344,22 +354,48 @@
     )(prefix_length, q, *[caches[r] for r in near], *[spans[r] for r in near])
     others = {rel: both for rel, both in held.items() if rel > 1}
     others, state = lax.optimization_barrier((others, state))
-    others.update(key_step(others, 1))
     caches.update({rel: in_vmem(both[0]) for rel, both in others.items()})
     spans.update({rel: in_vmem(both[1]) for rel, both in others.items()})
-    state = [in_vmem(x) for x in state]
+
+    def go_on(which, rels, state, last):
+        if last:
+            shapes = [pltpu.VMEM((rows, heads * DV), bf16)]
+        else:
+            shapes = [
+                pltpu.VMEM((1, heads, rows, KVL), f32),
+                pltpu.VMEM((1, heads, rows, LANES), f32),
+                pltpu.VMEM((1, heads, rows, LANES), f32),
+            ]
+        up = [in_vmem(w_uv)] if last else []
+        return pl.pallas_call(
+            functools.partial(step_kernel, rels, tokens, group, which, last),
+            in_specs=[smem] + [vmem] * (4 + len(up) + 2 * len(rels)),
+            out_specs=[vmem] * len(shapes),
+            out_shape=shapes,
+            scratch_shapes=key_scratch(rels),
+            compiler_params=params,
+            name="far_keys" if last else "counterpart_keys",
+            cost_estimate=cost(4 * rows * heads * len(rels) * (cache_rows + tokens) * KD),
+        )(
+            prefix_length,
+            q,
+            *[in_vmem(x) for x in state],
+            *up,
+            *[caches[r] for r in rels],
+            *[spans[r] for r in rels],
+        )
+
+    straight = [go_on(which, [r for r in far if r % 2 == 0], state, False) for which in range(AHEAD)]
+    crossed = key_step(others, 1)
+    if AHEAD:
+        crossed, straight = lax.optimization_barrier((crossed, straight))
+    caches.update({rel: in_vmem(both[0]) for rel, both in crossed.items()})
+    spans.update({rel: in_vmem(both[1]) for rel, both in crossed.items()})
 
     def rest(which):
-        return pl.pallas_call(
-            functools.partial(rest_kernel, far, tokens, group, which),
-            in_specs=[smem] + [vmem] * (5 + 2 * len(far)),
-            out_specs=vmem,
-            out_shape=pltpu.VMEM((rows, heads * DV), bf16),
-            scratch_shapes=key_scratch(far),
-            compiler_params=params,
-            name="far_keys",
-            cost_estimate=cost(4 * rows * heads * len(far) * (cache_rows + tokens) * KD),
-        )(prefix_length, q, *state, in_vmem(w_uv), *[caches[r] for r in far], *[spans[r] for r in far])
+        if which < AHEAD:
+            return go_on(which, [rel for rel in far if rel % 2], straight[which], True)[0]
+        return go_on(which, far, state, True)[0]
 
     columns = w_o.shape[1]
     depth = w_o.shape[0]

time: 64.9 us -> 63.9 us (0.985)
  waiting for transfers between devices: 25.8 us -> 22.7 us
  starting transfers between devices: 22.2 us -> 23.7 us
    ppermute x24, waiting for transfers between devices: 25.8 us -> 22.7 us  [xor_permute(): return lax.ppermute(x, axis, [(i, i ^ bit) for i in range(n)])]
    ppermute x24, starting transfers between devices: 22.2 us -> 23.7 us  [xor_permute(): return lax.ppermute(x, axis, [(i, i ^ bit) for i in range(n)])]
    pallas_call x2 -> x3, Pallas kernels: 4.85 us -> 5.5 us  [go_on(): pl.pallas_call(functools.partial(step_kernel, rels, tokens, group, which,...]
  transfers between devices with their start and end apart: 24 -> 24, of which waited for: 12 -> 10; matrix products, arithmetic and copies ran while one was open for 1% -> 1% of each run, Pallas kernels for 19% -> 21%
where the time goes in v3:
time: 63.9 us; the launch traced here: 63.7 us
  starting transfers between devices  23.7 us (37%)
  waiting for transfers between devices  22.7 us (36%)
  Pallas kernels  15.3 us (24%)
  other arithmetic  1.1 us (2%)
  between operations  0.9 us (1%)
    ppermute x24, starting transfers between devices, xor_permute(): return lax.ppermute(x, axis, [(i, i ^ bit) for i in range(n)])  23.7 us
    ppermute x24, waiting for transfers between devices, xor_permute(): return lax.ppermute(x, axis, [(i, i ^ bit) for i in range(n)])  22.7 us
    pallas_call x3, Pallas kernels, go_on(): pl.pallas_call(functools.partial(step_kernel, rels, tokens, group, which,...  5.5 us
    pallas_call x2, Pallas kernels, project(): pl.pallas_call(functools.partial(project_kernel, n_tok, per, groups), in_...  4.23 us
    pallas_call x1, Pallas kernels, shards(): pl.pallas_call(functools.partial(local_kernel, near, tokens, group), in_s...  3.03 us
    pallas_call x1, Pallas kernels, shards(): pl.pallas_call(functools.partial(query_kernel, tokens, group), in_specs=[...  2.59 us
  transfers between devices with their start and end apart: 24, of which 10 were waited for; matrix products, arithmetic and copies ran while one was open for 1% of the time, Pallas kernels for 21%

profile of v3, /device:TPU:0, one launch (start us, length us, event | category | flops | bytes accessed | tf_op | source)
XLA Modules:
  0.0 63.7 jit_solution(17757487720138621939)
XLA Ops:
  0.5 2.9 %collective-permute-start = (bf16[576,128]{1,0:T(8,128)(2,1)}, bf16[576,128]{1,0:T(8,128)(2,1)S(1)}, u32[]{:S(2)}, u32[]{:S(2)}) collective-permute-start(bf16[576,128]{1,0:T(8,128)(2,1)} %bitcast.5), channel_id=1, source_target_pairs={{0,16},{8,24},{16,0},{24,8},{1,17},{9,25},{17,1},{25,9},{2,18},{10... | collective-permute-start | bytes 442376 | tf_op jit(solution)/shard_map/ppermute | solution.py:44
  4.2 2.6 %query_latent.1.refs_1_ = bf16[2,16,64,640]{3,2,1,0:T(8,128)(2,1)S(1)} custom-call(bf16[128,2048]{1,0:T(8,128)(2,1)} %qn.1, bf16[128,1024]{1,0:T(8,128)(2,1)} %qr.1, bf16[512,2048]{1,0:T(8,128)(2,1)} %wuk.1), custom_call_target="tpu_custom_call" | custom-call | flops 268435456 | tf_op jit(solution)/shard_map/query_latent/pallas_call | solution.py:324
  6.8 3.0 %local_keys.1 = (f32[2,16,64,512]{3,2,1,0:T(8,128)S(1)}, f32[2,16,64,128]{3,2,1,0:T(8,128)S(1)}, f32[2,16,64,128]{3,2,1,0:T(8,128)S(1)}) custom-call(s32[1]{0:T(128)S(6)} %copy.9.refs_0_, bf16[2,16,64,640]{3,2,1,0:T(8,128)(2,1)S(1)} %query_latent.1.refs_1_, bf16[576,128]{1,0:T(8,128)(2,1)S(1)} %bitcast.6, ...), custom_call_target="tpu_custom_call" | custom-call | flops 2415919104 | tf_op jit(solution)/shard_map/local_keys/pallas_call | solution.py:341
  11.3 1.2 %counterpart_keys.1 = (f32[1,16,64,512]{3,2,1,0:T(8,128)S(1)}, f32[1,16,64,128]{3,2,1,0:T(8,128)S(1)}, f32[1,16,64,128]{3,2,1,0:T(8,128)S(1)}) custom-call(s32[1]{0:T(128)S(6)} %copy.9.refs_0_, bf16[2,16,64,640]{3,2,1,0:T(8,128)(2,1)S(1)} %query_latent.1.refs_1_, f32[2,16,64,512]{3,2,1,0:T(8,128)S(1)} %get-tuple-element.34.refs_2_, ...), custom_call_target="tpu_custom_call" | custom-call | flops 603979776 | tf_op jit(solution)/shard_map/counterpart_keys/pallas_call | solution.py:370
  12.6 1.9 %far_keys.2.refs_0_ = bf16[64,2048]{1,0:T(8,128)(2,1)S(1)} custom-call(s32[1]{0:T(128)S(6)} %copy.9.refs_0_, bf16[2,16,64,640]{3,2,1,0:T(8,128)(2,1)S(1)} %query_latent.1.refs_1_, f32[1,16,64,512]{3,2,1,0:T(8,128)S(1)} %get-tuple-element.40.refs_2_, f32[1,16,64,128]{3,2,1,0:T(8,128)S(1)} %get-tuple-element.41.refs_3_, ...), custom_call_target="tpu_custom_call" | custom-call | flops 603979776 | tf_op jit(solution)/shard_map/far_keys/pallas_call | solution.py:370
  14.5 1.8 %collective-permute-start.7 = (bf16[64,2048]{1,0:T(8,128)(2,1)S(1)}, bf16[64,2048]{1,0:T(8,128)(2,1)S(1)}, u32[]{:S(2)}, u32[]{:S(2)}) collective-permute-start(bf16[64,2048]{1,0:T(8,128)(2,1)S(1)} %far_keys.2.refs_0_), channel_id=1, source_target_pairs={{0,16},{8,24},{16,0},{24,8},{1,17},{9,25},{17,1},{25,9},{2,18},{10... | collective-permute-start | bytes 786440 | tf_op jit(solution)/shard_map/ppermute | solution.py:44
  16.3 2.4 %far_keys.3.refs_0_ = bf16[64,2048]{1,0:T(8,128)(2,1)S(1)} custom-call(s32[1]{0:T(128)S(6)} %copy.9.refs_0_, bf16[2,16,64,640]{3,2,1,0:T(8,128)(2,1)S(1)} %query_latent.1.refs_1_, f32[2,16,64,512]{3,2,1,0:T(8,128)S(1)} %get-tuple-element.34.refs_2_, f32[2,16,64,128]{3,2,1,0:T(8,128)S(1)} %get-tuple-element.35.refs_3_, ...), custom_call_target="tpu_custom_call" | custom-call | flops 1207959552 | tf_op jit(solution)/shard_map/far_keys/pallas_call | solution.py:370
  19.1 4.6 %collective-permute-done.7.refs_2_ = bf16[64,2048]{1,0:T(8,128)(2,1)S(1)} collective-permute-done((bf16[64,2048]{1,0:T(8,128)(2,1)S(1)}, bf16[64,2048]{1,0:T(8,128)(2,1)S(1)}, u32[]{:S(2)}, u32[]{:S(2)}) %collective-permute-start.7) | collective-permute-done | bytes 262176 | tf_op jit(solution)/shard_map/ppermute | solution.py:44
  24.2 4.3 %collective-permute-done.16.refs_2_ = bf16[64,2048]{1,0:T(8,128)(2,1)S(1)} collective-permute-done((bf16[64,2048]{1,0:T(8,128)(2,1)S(1)}, bf16[64,2048]{1,0:T(8,128)(2,1)S(1)}, u32[]{:S(2)}, u32[]{:S(2)}) %collective-permute-start.16) | collective-permute-done | bytes 262176 | tf_op jit(solution)/shard_map/ppermute | solution.py:44
  28.6 2.1 %project.2 = (bf16[128,1024]{1,0:T(8,128)(2,1)S(1)}, bf16[128,1024]{1,0:T(8,128)(2,1)S(1)}, bf16[128,768]{1,0:T(8,128)(2,1)S(1)}, bf16[128,768]{1,0:T(8,128)(2,1)S(1)}) custom-call(bf16[64,2048]{1,0:T(8,128)(2,1)S(1)} %far_keys.2.refs_0_, bf16[64,2048]{1,0:T(8,128)(2,1)S(1)} %collective-permute-done.6.refs_1_, ...), custom_call_target="tpu_custom_call" | custom-call | flops 1879048192 | tf_op jit(solution)/shard_map/project/pallas_call | solution.py:421
  30.7 1.9 %collective-permute-start.12 = (bf16[128,768]{1,0:T(8,128)(2,1)S(1)}, bf16[128,768]{1,0:T(8,128)(2,1)S(1)}, u32[]{:S(2)}, u32[]{:S(2)}) collective-permute-start(bf16[128,768]{1,0:T(8,128)(2,1)S(1)} %get-tuple-element.48), channel_id=1, source_target_pairs={{0,2},{1,3},{2,0},{3,1},{4,6},{5,7},{6,4},{7,5},{8,10},{9,11},{10,... | collective-permute-start | bytes 589832 | tf_op jit(solution)/shard_map/ppermute | solution.py:44
  32.6 1.5 %collective-permute-start.9 = (bf16[128,1024]{1,0:T(8,128)(2,1)S(1)}, bf16[128,1024]{1,0:T(8,128)(2,1)S(1)}, u32[]{:S(2)}, u32[]{:S(2)}) collective-permute-start(bf16[128,1024]{1,0:T(8,128)(2,1)S(1)} %get-tuple-element.46), channel_id=1, source_target_pairs={{0,1},{1,0},{2,3},{3,2},{4,5},{5,4},{6,7},{7,6},{8,9},{9,8},{10,11... | collective-permute-start | bytes 786440 | tf_op jit(solution)/shard_map/ppermute | solution.py:44
  34.1 2.1 %project.3 = (bf16[128,1024]{1,0:T(8,128)(2,1)S(1)}, bf16[128,1024]{1,0:T(8,128)(2,1)S(1)}, bf16[128,768]{1,0:T(8,128)(2,1)S(1)}, bf16[128,768]{1,0:T(8,128)(2,1)S(1)}) custom-call(bf16[64,2048]{1,0:T(8,128)(2,1)S(1)} %far_keys.3.refs_0_, bf16[64,2048]{1,0:T(8,128)(2,1)S(1)} %collective-permute-done.15.refs_1_, ...), custom_call_target="tpu_custom_call" | custom-call | flops 1879048192 | tf_op jit(solution)/shard_map/project/pallas_call | solution.py:421
  38.2 2.8 %collective-permute-start.13 = (bf16[64,768]{1,0:T(8,128)(2,1)S(1)}, bf16[64,768]{1,0:T(8,128)(2,1)S(1)}, u32[]{:S(2)}, u32[]{:S(2)}) collective-permute-start(bf16[64,768]{1,0:T(8,128)(2,1)S(1)} %get-tuple-element.58), channel_id=1, source_target_pairs={{0,4},{1,5},{2,6},{3,7},{4,0},{5,1},{6,2},{7,3},{8,12},{9,13},{10,... | collective-permute-start | bytes 294920 | tf_op jit(solution)/shard_map/ppermute | solution.py:44
  41.0 4.4 %collective-permute-done.21 = bf16[128,768]{1,0:T(8,128)(2,1)S(1)} collective-permute-done((bf16[128,768]{1,0:T(8,128)(2,1)S(1)}, bf16[128,768]{1,0:T(8,128)(2,1)S(1)}, u32[]{:S(2)}, u32[]{:S(2)}) %collective-permute-start.21) | collective-permute-done | bytes 196640 | tf_op jit(solution)/shard_map/ppermute | solution.py:44
  45.4 1.6 %collective-permute-start.22 = (bf16[64,768]{1,0:T(8,128)(2,1)S(1)}, bf16[64,768]{1,0:T(8,128)(2,1)S(1)}, u32[]{:S(2)}, u32[]{:S(2)}) collective-permute-start(bf16[64,768]{1,0:T(8,128)(2,1)S(1)} %get-tuple-element.60), channel_id=1, source_target_pairs={{0,4},{1,5},{2,6},{3,7},{4,0},{5,1},{6,2},{7,3},{8,12},{9,13},{10,... | collective-permute-start | bytes 294920 | tf_op jit(solution)/shard_map/ppermute | solution.py:44
  47.8 1.5 %collective-permute-start.19 = (bf16[64,1024]{1,0:T(8,128)(2,1)S(1)}, bf16[64,1024]{1,0:T(8,128)(2,1)S(1)}, u32[]{:S(2)}, u32[]{:S(2)}) collective-permute-start(bf16[64,1024]{1,0:T(8,128)(2,1)S(1)} %get-tuple-element.56), channel_id=1, source_target_pairs={{0,2},{1,3},{2,0},{3,1},{4,6},{5,7},{6,4},{7,5},{8,10},{9,11},{10,... | collective-permute-start | bytes 393224 | tf_op jit(solution)/shard_map/ppermute | solution.py:44
  49.4 1.6 %collective-permute-start.14 = (bf16[32,768]{1,0:T(8,128)(2,1)S(1)}, bf16[32,768]{1,0:T(8,128)(2,1)S(1)}, u32[]{:S(2)}, u32[]{:S(2)}) collective-permute-start(bf16[32,768]{1,0:T(8,128)(2,1)S(1)} %add_convert_fusion.18), channel_id=1, source_target_pairs={{0,1},{1,0},{2,3},{3,2},{4,5},{5,4},{6,7},{7,6},{8,9},{9,8},{10,11... | collective-permute-start | bytes 147464 | tf_op jit(solution)/shard_map/ppermute | solution.py:44
  51.7 1.6 %collective-permute-start.23 = (bf16[32,768]{1,0:T(8,128)(2,1)S(1)}, bf16[32,768]{1,0:T(8,128)(2,1)S(1)}, u32[]{:S(2)}, u32[]{:S(2)}) collective-permute-start(bf16[32,768]{1,0:T(8,128)(2,1)S(1)} %add_convert_fusion.15), channel_id=1, source_target_pairs={{0,1},{1,0},{2,3},{3,2},{4,5},{5,4},{6,7},{7,6},{8,9},{9,8},{10,11... | collective-permute-start | bytes 147464 | tf_op jit(solution)/shard_map/ppermute | solution.py:44
  53.9 1.9 %collective-permute-done.23 = bf16[32,768]{1,0:T(8,128)(2,1)S(1)} collective-permute-done((bf16[32,768]{1,0:T(8,128)(2,1)S(1)}, bf16[32,768]{1,0:T(8,128)(2,1)S(1)}, u32[]{:S(2)}, u32[]{:S(2)}) %collective-permute-start.23) | collective-permute-done | bytes 49184 | tf_op jit(solution)/shard_map/ppermute | solution.py:44
  55.9 1.6 %collective-permute-start.11 = (bf16[32,1024]{1,0:T(8,128)(2,1)S(1)}, bf16[32,1024]{1,0:T(8,128)(2,1)S(1)}, u32[]{:S(2)}, u32[]{:S(2)}) collective-permute-start(bf16[32,1024]{1,0:T(8,128)(2,1)S(1)} %add_convert_fusion.12), channel_id=1, source_target_pairs={{0,4},{1,5},{2,6},{3,7},{4,0},{5,1},{6,2},{7,3},{8,12},{9,13},{10,... | collective-permute-start | bytes 196616 | tf_op jit(solution)/shard_map/ppermute | solution.py:44
  57.5 1.5 %collective-permute-start.20 = (bf16[32,1024]{1,0:T(8,128)(2,1)S(1)}, bf16[32,1024]{1,0:T(8,128)(2,1)S(1)}, u32[]{:S(2)}, u32[]{:S(2)}) collective-permute-start(bf16[32,1024]{1,0:T(8,128)(2,1)S(1)} %add_convert_fusion.9), channel_id=1, source_target_pairs={{0,4},{1,5},{2,6},{3,7},{4,0},{5,1},{6,2},{7,3},{8,12},{9,13},{10,... | collective-permute-start | bytes 196616 | tf_op jit(solution)/shard_map/ppermute | solution.py:44
  59.0 2.3 %collective-permute-done.11 = bf16[32,1024]{1,0:T(8,128)(2,1)S(1)} collective-permute-done((bf16[32,1024]{1,0:T(8,128)(2,1)S(1)}, bf16[32,1024]{1,0:T(8,128)(2,1)S(1)}, u32[]{:S(2)}, u32[]{:S(2)}) %collective-permute-start.11) | collective-permute-done | bytes 65568 | tf_op jit(solution)/shard_map/ppermute | solution.py:44
  61.3 1.7 %collective-permute-done.20 = bf16[32,1024]{1,0:T(8,128)(2,1)S(1)} collective-permute-done((bf16[32,1024]{1,0:T(8,128)(2,1)S(1)}, bf16[32,1024]{1,0:T(8,128)(2,1)S(1)}, u32[]{:S(2)}, u32[]{:S(2)}) %collective-permute-start.20) | collective-permute-done | bytes 65568 | tf_op jit(solution)/shard_map/ppermute | solution.py:44
  (55 shorter events, 8.0 us)
Async XLA Ops:
  0.0 6.8 %collective-permute-start.2 = (bf16[576,128]{1,0:T(8,128)(2,1)}, bf16[576,128]{1,0:T(8,128)(2,1)S(1)}, u32[]{:S(2)}, u32[]{:S(2)}) collective-permute-start(bf16[576,128]{1,0:T(8,128)(2,1)} %bitcast.4), channel_id=1, source_target_pairs={{0,8},{8,0},{16,24},{24,16},{1,9},{9,1},{17,25},{25,17},{2,10},{10... | collective-permute-start | bytes 442376 | tf_op jit(solution)/shard_map/ppermute | solution.py:44
  0.5 6.3 %collective-permute-start.3 = (bf16[576,128]{1,0:T(8,128)(2,1)}, bf16[576,128]{1,0:T(8,128)(2,1)S(1)}, u32[]{:S(2)}, u32[]{:S(2)}) collective-permute-start(bf16[576,128]{1,0:T(8,128)(2,1)} %bitcast.7), channel_id=1, source_target_pairs={{0,8},{8,0},{16,24},{24,16},{1,9},{9,1},{17,25},{25,17},{2,10},{10... | collective-permute-start | bytes 442376 | tf_op jit(solution)/shard_map/ppermute | solution.py:44
  0.5 9.3 %collective-permute-start = (bf16[576,128]{1,0:T(8,128)(2,1)}, bf16[576,128]{1,0:T(8,128)(2,1)S(1)}, u32[]{:S(2)}, u32[]{:S(2)}) collective-permute-start(bf16[576,128]{1,0:T(8,128)(2,1)} %bitcast.5), channel_id=1, source_target_pairs={{0,16},{8,24},{16,0},{24,8},{1,17},{9,25},{17,1},{25,9},{2,18},{10... | collective-permute-start | bytes 442376 | tf_op jit(solution)/shard_map/ppermute | solution.py:44
  3.5 7.4 %collective-permute-start.1 = (bf16[576,128]{1,0:T(8,128)(2,1)}, bf16[576,128]{1,0:T(8,128)(2,1)S(1)}, u32[]{:S(2)}, u32[]{:S(2)}) collective-permute-start(bf16[576,128]{1,0:T(8,128)(2,1)} %bitcast.8), channel_id=1, source_target_pairs={{0,16},{8,24},{16,0},{24,8},{1,17},{9,25},{17,1},{25,9},{2,18},{10... | collective-permute-start | bytes 442376 | tf_op jit(solution)/shard_map/ppermute | solution.py:44
  10.8 1.7 %collective-permute-start.4 = (bf16[576,128]{1,0:T(8,128)(2,1)S(1)}, bf16[576,128]{1,0:T(8,128)(2,1)S(1)}, u32[]{:S(2)}, u32[]{:S(2)}) collective-permute-start(bf16[576,128]{1,0:T(8,128)(2,1)S(1)} %collective-permute-done.refs_5_.refs_6_), channel_id=1, source_target_pairs={{0,8},{8,0},{16,24},{24,16},{1,9},{9,1},{17,25},{25,17},{2,10},{10... | collective-permute-start | bytes 442376 | tf_op jit(solution)/shard_map/ppermute | solution.py:44
  10.8 1.7 %collective-permute-start.5 = (bf16[576,128]{1,0:T(8,128)(2,1)S(1)}, bf16[576,128]{1,0:T(8,128)(2,1)S(1)}, u32[]{:S(2)}, u32[]{:S(2)}) collective-permute-start(bf16[576,128]{1,0:T(8,128)(2,1)S(1)} %collective-permute-done.1.refs_6_.refs_8_), channel_id=1, source_target_pairs={{0,8},{8,0},{16,24},{24,16},{1,9},{9,1},{17,25},{25,17},{2,10},{10... | collective-permute-start | bytes 442376 | tf_op jit(solution)/shard_map/ppermute | solution.py:44
  14.5 9.2 %collective-permute-start.7 = (bf16[64,2048]{1,0:T(8,128)(2,1)S(1)}, bf16[64,2048]{1,0:T(8,128)(2,1)S(1)}, u32[]{:S(2)}, u32[]{:S(2)}) collective-permute-start(bf16[64,2048]{1,0:T(8,128)(2,1)S(1)} %far_keys.2.refs_0_), channel_id=1, source_target_pairs={{0,16},{8,24},{16,0},{24,8},{1,17},{9,25},{17,1},{25,9},{2,18},{10... | collective-permute-start | bytes 786440 | tf_op jit(solution)/shard_map/ppermute | solution.py:44
  18.7 9.8 %collective-permute-start.16 = (bf16[64,2048]{1,0:T(8,128)(2,1)S(1)}, bf16[64,2048]{1,0:T(8,128)(2,1)S(1)}, u32[]{:S(2)}, u32[]{:S(2)}) collective-permute-start(bf16[64,2048]{1,0:T(8,128)(2,1)S(1)} %far_keys.3.refs_0_), channel_id=1, source_target_pairs={{0,16},{8,24},{16,0},{24,8},{1,17},{9,25},{17,1},{25,9},{2,18},{10... | collective-permute-start | bytes 786440 | tf_op jit(solution)/shard_map/ppermute | solution.py:44
  19.1 9.5 %collective-permute-start.6 = (bf16[64,2048]{1,0:T(8,128)(2,1)S(1)}, bf16[64,2048]{1,0:T(8,128)(2,1)S(1)}, u32[]{:S(2)}, u32[]{:S(2)}) collective-permute-start(bf16[64,2048]{1,0:T(8,128)(2,1)S(1)} %far_keys.2.refs_0_), channel_id=1, source_target_pairs={{0,8},{8,0},{16,24},{24,16},{1,9},{9,1},{17,25},{25,17},{2,10},{10... | collective-permute-start | bytes 786440 | tf_op jit(solution)/shard_map/ppermute | solution.py:44
  23.7 4.8 %collective-permute-start.8 = (bf16[64,2048]{1,0:T(8,128)(2,1)S(1)}, bf16[64,2048]{1,0:T(8,128)(2,1)S(1)}, u32[]{:S(2)}, u32[]{:S(2)}) collective-permute-start(bf16[64,2048]{1,0:T(8,128)(2,1)S(1)} %collective-permute-done.7.refs_2_), channel_id=1, source_target_pairs={{0,8},{8,0},{16,24},{24,16},{1,9},{9,1},{17,25},{25,17},{2,10},{10... | collective-permute-start | bytes 786440 | tf_op jit(solution)/shard_map/ppermute | solution.py:44
  23.7 10.4 %collective-permute-start.15 = (bf16[64,2048]{1,0:T(8,128)(2,1)S(1)}, bf16[64,2048]{1,0:T(8,128)(2,1)S(1)}, u32[]{:S(2)}, u32[]{:S(2)}) collective-permute-start(bf16[64,2048]{1,0:T(8,128)(2,1)S(1)} %far_keys.3.refs_0_), channel_id=1, source_target_pairs={{0,8},{8,0},{16,24},{24,16},{1,9},{9,1},{17,25},{25,17},{2,10},{10... | collective-permute-start | bytes 786440 | tf_op jit(solution)/shard_map/ppermute | solution.py:44
  28.5 5.6 %collective-permute-start.17 = (bf16[64,2048]{1,0:T(8,128)(2,1)S(1)}, bf16[64,2048]{1,0:T(8,128)(2,1)S(1)}, u32[]{:S(2)}, u32[]{:S(2)}) collective-permute-start(bf16[64,2048]{1,0:T(8,128)(2,1)S(1)} %collective-permute-done.16.refs_2_), channel_id=1, source_target_pairs={{0,8},{8,0},{16,24},{24,16},{1,9},{9,1},{17,25},{25,17},{2,10},{10... | collective-permute-start | bytes 786440 | tf_op jit(solution)/shard_map/ppermute | solution.py:44
  30.7 7.5 %collective-permute-start.12 = (bf16[128,768]{1,0:T(8,128)(2,1)S(1)}, bf16[128,768]{1,0:T(8,128)(2,1)S(1)}, u32[]{:S(2)}, u32[]{:S(2)}) collective-permute-start(bf16[128,768]{1,0:T(8,128)(2,1)S(1)} %get-tuple-element.48), channel_id=1, source_target_pairs={{0,2},{1,3},{2,0},{3,1},{4,6},{5,7},{6,4},{7,5},{8,10},{9,11},{10,... | collective-permute-start | bytes 589832 | tf_op jit(solution)/shard_map/ppermute | solution.py:44
  32.6 14.4 %collective-permute-start.9 = (bf16[128,1024]{1,0:T(8,128)(2,1)S(1)}, bf16[128,1024]{1,0:T(8,128)(2,1)S(1)}, u32[]{:S(2)}, u32[]{:S(2)}) collective-permute-start(bf16[128,1024]{1,0:T(8,128)(2,1)S(1)} %get-tuple-element.46), channel_id=1, source_target_pairs={{0,1},{1,0},{2,3},{3,2},{4,5},{5,4},{6,7},{7,6},{8,9},{9,8},{10,11... | collective-permute-start | bytes 786440 | tf_op jit(solution)/shard_map/ppermute | solution.py:44
  36.2 11.5 %collective-permute-start.18 = (bf16[128,1024]{1,0:T(8,128)(2,1)S(1)}, bf16[128,1024]{1,0:T(8,128)(2,1)S(1)}, u32[]{:S(2)}, u32[]{:S(2)}) collective-permute-start(bf16[128,1024]{1,0:T(8,128)(2,1)S(1)} %get-tuple-element.50), channel_id=1, source_target_pairs={{0,1},{1,0},{2,3},{3,2},{4,5},{5,4},{6,7},{7,6},{8,9},{9,8},{10,11... | collective-permute-start | bytes 786440 | tf_op jit(solution)/shard_map/ppermute | solution.py:44
  36.8 8.6 %collective-permute-start.21 = (bf16[128,768]{1,0:T(8,128)(2,1)S(1)}, bf16[128,768]{1,0:T(8,128)(2,1)S(1)}, u32[]{:S(2)}, u32[]{:S(2)}) collective-permute-start(bf16[128,768]{1,0:T(8,128)(2,1)S(1)} %get-tuple-element.52), channel_id=1, source_target_pairs={{0,2},{1,3},{2,0},{3,1},{4,6},{5,7},{6,4},{7,5},{8,10},{9,11},{10,... | collective-permute-start | bytes 589832 | tf_op jit(solution)/shard_map/ppermute | solution.py:44
  38.2 11.1 %collective-permute-start.13 = (bf16[64,768]{1,0:T(8,128)(2,1)S(1)}, bf16[64,768]{1,0:T(8,128)(2,1)S(1)}, u32[]{:S(2)}, u32[]{:S(2)}) collective-permute-start(bf16[64,768]{1,0:T(8,128)(2,1)S(1)} %get-tuple-element.58), channel_id=1, source_target_pairs={{0,4},{1,5},{2,6},{3,7},{4,0},{5,1},{6,2},{7,3},{8,12},{9,13},{10,... | collective-permute-start | bytes 294920 | tf_op jit(solution)/shard_map/ppermute | solution.py:44
  45.4 6.2 %collective-permute-start.22 = (bf16[64,768]{1,0:T(8,128)(2,1)S(1)}, bf16[64,768]{1,0:T(8,128)(2,1)S(1)}, u32[]{:S(2)}, u32[]{:S(2)}) collective-permute-start(bf16[64,768]{1,0:T(8,128)(2,1)S(1)} %get-tuple-element.60), channel_id=1, source_target_pairs={{0,4},{1,5},{2,6},{3,7},{4,0},{5,1},{6,2},{7,3},{8,12},{9,13},{10,... | collective-permute-start | bytes 294920 | tf_op jit(solution)/shard_map/ppermute | solution.py:44
  47.1 8.8 %collective-permute-start.10 = (bf16[64,1024]{1,0:T(8,128)(2,1)S(1)}, bf16[64,1024]{1,0:T(8,128)(2,1)S(1)}, u32[]{:S(2)}, u32[]{:S(2)}) collective-permute-start(bf16[64,1024]{1,0:T(8,128)(2,1)S(1)} %get-tuple-element.54), channel_id=1, source_target_pairs={{0,2},{1,3},{2,0},{3,1},{4,6},{5,7},{6,4},{7,5},{8,10},{9,11},{10,... | collective-permute-start | bytes 393224 | tf_op jit(solution)/shard_map/ppermute | solution.py:44
  47.8 9.6 %collective-permute-start.19 = (bf16[64,1024]{1,0:T(8,128)(2,1)S(1)}, bf16[64,1024]{1,0:T(8,128)(2,1)S(1)}, u32[]{:S(2)}, u32[]{:S(2)}) collective-permute-start(bf16[64,1024]{1,0:T(8,128)(2,1)S(1)} %get-tuple-element.56), channel_id=1, source_target_pairs={{0,2},{1,3},{2,0},{3,1},{4,6},{5,7},{6,4},{7,5},{8,10},{9,11},{10,... | collective-permute-start | bytes 393224 | tf_op jit(solution)/shard_map/ppermute | solution.py:44
  49.4 4.6 %collective-permute-start.14 = (bf16[32,768]{1,0:T(8,128)(2,1)S(1)}, bf16[32,768]{1,0:T(8,128)(2,1)S(1)}, u32[]{:S(2)}, u32[]{:S(2)}) collective-permute-start(bf16[32,768]{1,0:T(8,128)(2,1)S(1)} %add_convert_fusion.18), channel_id=1, source_target_pairs={{0,1},{1,0},{2,3},{3,2},{4,5},{5,4},{6,7},{7,6},{8,9},{9,8},{10,11... | collective-permute-start | bytes 147464 | tf_op jit(solution)/shard_map/ppermute | solution.py:44
  51.7 4.2 %collective-permute-start.23 = (bf16[32,768]{1,0:T(8,128)(2,1)S(1)}, bf16[32,768]{1,0:T(8,128)(2,1)S(1)}, u32[]{:S(2)}, u32[]{:S(2)}) collective-permute-start(bf16[32,768]{1,0:T(8,128)(2,1)S(1)} %add_convert_fusion.15), channel_id=1, source_target_pairs={{0,1},{1,0},{2,3},{3,2},{4,5},{5,4},{6,7},{7,6},{8,9},{9,8},{10,11... | collective-permute-start | bytes 147464 | tf_op jit(solution)/shard_map/ppermute | solution.py:44
  55.9 5.4 %collective-permute-start.11 = (bf16[32,1024]{1,0:T(8,128)(2,1)S(1)}, bf16[32,1024]{1,0:T(8,128)(2,1)S(1)}, u32[]{:S(2)}, u32[]{:S(2)}) collective-permute-start(bf16[32,1024]{1,0:T(8,128)(2,1)S(1)} %add_convert_fusion.12), channel_id=1, source_target_pairs={{0,4},{1,5},{2,6},{3,7},{4,0},{5,1},{6,2},{7,3},{8,12},{9,13},{10,... | collective-permute-start | bytes 196616 | tf_op jit(solution)/shard_map/ppermute | solution.py:44
  57.5 5.5 %collective-permute-start.20 = (bf16[32,1024]{1,0:T(8,128)(2,1)S(1)}, bf16[32,1024]{1,0:T(8,128)(2,1)S(1)}, u32[]{:S(2)}, u32[]{:S(2)}) collective-permute-start(bf16[32,1024]{1,0:T(8,128)(2,1)S(1)} %add_convert_fusion.9), channel_id=1, source_target_pairs={{0,4},{1,5},{2,6},{3,7},{4,0},{5,1},{6,2},{7,3},{8,12},{9,13},{10,... | collective-permute-start | bytes 196616 | tf_op jit(solution)/shard_map/ppermute | solution.py:44
  (5 other events, 37.0 us)

commit v4 on v3

--- a/solution.py
+++ b/solution.py
@@ -23,7 +23,7 @@
     (0.43, lambda bits: [(b,) for b in bits[1:] + bits[:1]]),
 )
 COST_SHARE = 1
-AHEAD = 1
+AHEAD = 2
 VMEM_LIMIT = 24 * 1024 * 1024
 EXP_SCALE = math.log2(math.e) / math.sqrt(DN + DR)
 
@@ -270,6 +270,15 @@
             y = jnp.concatenate([y[r * part : (r + 1) * part] for r in order], 0)
             for j, out in enumerate(mine):
                 out[:, here] = y[j * rows : (j + 1) * rows]
+
+
+def join_kernel(places, *refs):
+    *terms, out = refs
+    for row, column, count in places:
+        mine, terms = terms[:count], terms[count:]
+        height, width = mine[0].shape
+        total = sum(x[...].astype(f32) for x in mine)
+        out[row : row + height, column : column + width] = total.astype(bf16)
 
 
 def shards(q_nope, q_rope, cache_kv, span_kv, w_uk, w_uv, w_o, prefix_length):
@@ -388,7 +397,7 @@
     straight = [go_on(which, [r for r in far if r % 2 == 0], state, False) for which in range(AHEAD)]
     crossed = key_step(others, 1)
     if AHEAD:
-        crossed, straight = lax.optimization_barrier((crossed, straight))
+        crossed, straight[0] = lax.optimization_barrier((crossed, straight[0]))
     caches.update({rel: in_vmem(both[0]) for rel, both in crossed.items()})
     spans.update({rel: in_vmem(both[1]) for rel, both in crossed.items()})
 
@@ -434,24 +443,32 @@
             moves = combinations(bits)[:-1]
             got = [xor_permute(x, "head", move) for x, move in zip(parts, moves)]
             terms = [parts[-1]] + got
-            ways = len(combinations(stages[at + 1])) if at + 1 < len(stages) else 1
-            size = terms[0].shape[0] // ways
-            parts = [
-                sum(x[j * size : (j + 1) * size].astype(f32) for x in terms).astype(bf16)
-                for j in range(ways)
-            ]
-        return parts[0]
-
-    out = []
+            if at + 1 < len(stages):
+                ways = len(combinations(stages[at + 1]))
+                size = terms[0].shape[0] // ways
+                parts = [
+                    sum(x[j * size : (j + 1) * size].astype(f32) for x in terms).astype(bf16)
+                    for j in range(ways)
+                ]
+        return terms
+
+    places, terms = [], []
     for which in range(CHUNKS):
         parts = list(project(gather(rest(which))))
-        ends = []
-        for stages, _, _, _ in groups:
+        for stages, start, count, _ in groups:
             ways = len(combinations(stages[0]))
-            ends.append(scatter(parts[:ways], stages))
+            found = scatter(parts[:ways], stages)
+            places.append((which * (rows // per), start * tile, len(found)))
+            terms += found
             parts = parts[ways:]
-        out.append(jnp.concatenate(ends, 1))
-    return jnp.concatenate(out, 0)
+    return pl.pallas_call(
+        functools.partial(join_kernel, places),
+        in_specs=[vmem] * len(terms),
+        out_specs=vmem,
+        out_shape=jax.ShapeDtypeStruct((CHUNKS * (rows // per), columns), bf16),
+        compiler_params=params,
+        name="join",
+    )(*[in_vmem(x) for x in terms])
 
 
 def solution(mesh):

time: 63.9 us -> 62.5 us (0.978)
  Pallas kernels: 15.3 us -> 16.7 us
  waiting for transfers between devices: 22.7 us -> 21.4 us
  starting transfers between devices: 23.7 us -> 22.9 us
  other arithmetic: 1.1 us -> 0.35 us
    ppermute x24, waiting for transfers between devices: 22.7 us -> 21.4 us  [xor_permute(): return lax.ppermute(x, axis, [(i, i ^ bit) for i in range(n)])]
    pallas_call x0 -> x1, Pallas kernels: none -> 0.74 us  [shards(): pl.pallas_call(functools.partial(join_kernel, places), in_specs=[vmem] *...]
    ppermute x24, starting transfers between devices: 23.7 us -> 22.9 us  [xor_permute(): return lax.ppermute(x, axis, [(i, i ^ bit) for i in range(n)])]
    concatenate x1 -> x0, other arithmetic: 0.71 us -> none  [shards(): return jnp.concatenate(out, 0)]
    pallas_call x3 -> x4, Pallas kernels: 5.5 us -> 6.15 us  [go_on(): pl.pallas_call(functools.partial(step_kernel, rels, tokens, group, which,...]
  transfers between devices with their start and end apart: 24 -> 24, of which waited for: 10 -> 8; matrix products, arithmetic and copies ran while one was open for 1% -> 1% of each run, Pallas kernels for 21% -> 23%
where the time goes in v4:
time: 62.5 us; the launch traced here: 62.3 us
  starting transfers between devices  22.9 us (37%)
  waiting for transfers between devices  21.4 us (34%)
  Pallas kernels  16.7 us (27%)
  between operations  0.89 us (1%)
    ppermute x24, starting transfers between devices, xor_permute(): return lax.ppermute(x, axis, [(i, i ^ bit) for i in range(n)])  22.9 us
    ppermute x24, waiting for transfers between devices, xor_permute(): return lax.ppermute(x, axis, [(i, i ^ bit) for i in range(n)])  21.4 us
    pallas_call x4, Pallas kernels, go_on(): pl.pallas_call(functools.partial(step_kernel, rels, tokens, group, which,...  6.15 us
    pallas_call x2, Pallas kernels, project(): pl.pallas_call(functools.partial(project_kernel, n_tok, per, groups), in_...  4.23 us
    pallas_call x1, Pallas kernels, shards(): pl.pallas_call(functools.partial(local_kernel, near, tokens, group), in_s...  3.03 us
    pallas_call x1, Pallas kernels, shards(): pl.pallas_call(functools.partial(query_kernel, tokens, group), in_specs=[...  2.59 us
  transfers between devices with their start and end apart: 24, of which 8 were waited for; matrix products, arithmetic and copies ran while one was open for 1% of the time, Pallas kernels for 23%

profile of v4, /device:TPU:0, one launch (start us, length us, event | category | flops | bytes accessed | tf_op | source)
XLA Modules:
  0.0 62.3 jit_solution(2031450600602002603)
XLA Ops:
  0.5 2.9 %collective-permute-start = (bf16[576,128]{1,0:T(8,128)(2,1)}, bf16[576,128]{1,0:T(8,128)(2,1)S(1)}, u32[]{:S(2)}, u32[]{:S(2)}) collective-permute-start(bf16[576,128]{1,0:T(8,128)(2,1)} %bitcast.5), channel_id=1, source_target_pairs={{0,16},{8,24},{16,0},{24,8},{1,17},{9,25},{17,1},{25,9},{2,18},{10... | collective-permute-start | bytes 442376 | tf_op jit(solution)/shard_map/ppermute | solution.py:44
  4.2 2.6 %query_latent.1.refs_1_ = bf16[2,16,64,640]{3,2,1,0:T(8,128)(2,1)S(1)} custom-call(bf16[128,2048]{1,0:T(8,128)(2,1)} %qn.1, bf16[128,1024]{1,0:T(8,128)(2,1)} %qr.1, bf16[512,2048]{1,0:T(8,128)(2,1)} %wuk.1), custom_call_target="tpu_custom_call" | custom-call | flops 268435456 | tf_op jit(solution)/shard_map/query_latent/pallas_call | solution.py:333
  6.8 3.0 %local_keys.1 = (f32[2,16,64,512]{3,2,1,0:T(8,128)S(1)}, f32[2,16,64,128]{3,2,1,0:T(8,128)S(1)}, f32[2,16,64,128]{3,2,1,0:T(8,128)S(1)}) custom-call(s32[1]{0:T(128)S(6)} %copy.9.refs_0_, bf16[2,16,64,640]{3,2,1,0:T(8,128)(2,1)S(1)} %query_latent.1.refs_1_, bf16[576,128]{1,0:T(8,128)(2,1)S(1)} %bitcast.6, ...), custom_call_target="tpu_custom_call" | custom-call | flops 2415919104 | tf_op jit(solution)/shard_map/local_keys/pallas_call | solution.py:350
  11.3 1.2 %counterpart_keys.2 = (f32[1,16,64,512]{3,2,1,0:T(8,128)S(1)}, f32[1,16,64,128]{3,2,1,0:T(8,128)S(1)}, f32[1,16,64,128]{3,2,1,0:T(8,128)S(1)}) custom-call(s32[1]{0:T(128)S(6)} %copy.9.refs_0_, bf16[2,16,64,640]{3,2,1,0:T(8,128)(2,1)S(1)} %query_latent.1.refs_1_, f32[2,16,64,512]{3,2,1,0:T(8,128)S(1)} %get-tuple-element.37.refs_2_, ...), custom_call_target="tpu_custom_call" | custom-call | flops 603979776 | tf_op jit(solution)/shard_map/counterpart_keys/pallas_call | solution.py:379
  12.6 1.9 %far_keys.2.refs_0_ = bf16[64,2048]{1,0:T(8,128)(2,1)S(1)} custom-call(s32[1]{0:T(128)S(6)} %copy.9.refs_0_, bf16[2,16,64,640]{3,2,1,0:T(8,128)(2,1)S(1)} %query_latent.1.refs_1_, f32[1,16,64,512]{3,2,1,0:T(8,128)S(1)} %get-tuple-element.43.refs_2_, f32[1,16,64,128]{3,2,1,0:T(8,128)S(1)} %get-tuple-element.44.refs_3_, ...), custom_call_target="tpu_custom_call" | custom-call | flops 603979776 | tf_op jit(solution)/shard_map/far_keys/pallas_call | solution.py:379
  14.5 1.8 %collective-permute-start.7 = (bf16[64,2048]{1,0:T(8,128)(2,1)S(1)}, bf16[64,2048]{1,0:T(8,128)(2,1)S(1)}, u32[]{:S(2)}, u32[]{:S(2)}) collective-permute-start(bf16[64,2048]{1,0:T(8,128)(2,1)S(1)} %far_keys.2.refs_0_), channel_id=1, source_target_pairs={{0,16},{8,24},{16,0},{24,8},{1,17},{9,25},{17,1},{25,9},{2,18},{10... | collective-permute-start | bytes 786440 | tf_op jit(solution)/shard_map/ppermute | solution.py:44
  16.3 1.2 %counterpart_keys.3 = (f32[1,16,64,512]{3,2,1,0:T(8,128)S(1)}, f32[1,16,64,128]{3,2,1,0:T(8,128)S(1)}, f32[1,16,64,128]{3,2,1,0:T(8,128)S(1)}) custom-call(s32[1]{0:T(128)S(6)} %copy.9.refs_0_, bf16[2,16,64,640]{3,2,1,0:T(8,128)(2,1)S(1)} %query_latent.1.refs_1_, f32[2,16,64,512]{3,2,1,0:T(8,128)S(1)} %get-tuple-element.37.refs_2_, ...), custom_call_target="tpu_custom_call" | custom-call | flops 603979776 | tf_op jit(solution)/shard_map/counterpart_keys/pallas_call | solution.py:379
  17.5 1.9 %far_keys.3.refs_0_ = bf16[64,2048]{1,0:T(8,128)(2,1)S(1)} custom-call(s32[1]{0:T(128)S(6)} %copy.9.refs_0_, bf16[2,16,64,640]{3,2,1,0:T(8,128)(2,1)S(1)} %query_latent.1.refs_1_, f32[1,16,64,512]{3,2,1,0:T(8,128)S(1)} %get-tuple-element.52.refs_2_, f32[1,16,64,128]{3,2,1,0:T(8,128)S(1)} %get-tuple-element.53.refs_3_, ...), custom_call_target="tpu_custom_call" | custom-call | flops 603979776 | tf_op jit(solution)/shard_map/far_keys/pallas_call | solution.py:379
  19.7 4.0 %collective-permute-done.7.refs_2_ = bf16[64,2048]{1,0:T(8,128)(2,1)S(1)} collective-permute-done((bf16[64,2048]{1,0:T(8,128)(2,1)S(1)}, bf16[64,2048]{1,0:T(8,128)(2,1)S(1)}, u32[]{:S(2)}, u32[]{:S(2)}) %collective-permute-start.7) | collective-permute-done | bytes 262176 | tf_op jit(solution)/shard_map/ppermute | solution.py:44
  24.2 4.3 %collective-permute-done.16.refs_2_ = bf16[64,2048]{1,0:T(8,128)(2,1)S(1)} collective-permute-done((bf16[64,2048]{1,0:T(8,128)(2,1)S(1)}, bf16[64,2048]{1,0:T(8,128)(2,1)S(1)}, u32[]{:S(2)}, u32[]{:S(2)}) %collective-permute-start.16) | collective-permute-done | bytes 262176 | tf_op jit(solution)/shard_map/ppermute | solution.py:44
  28.6 2.1 %project.2 = (bf16[128,1024]{1,0:T(8,128)(2,1)S(1)}, bf16[128,1024]{1,0:T(8,128)(2,1)S(1)}, bf16[128,768]{1,0:T(8,128)(2,1)S(1)}, bf16[128,768]{1,0:T(8,128)(2,1)S(1)}) custom-call(bf16[64,2048]{1,0:T(8,128)(2,1)S(1)} %far_keys.2.refs_0_, bf16[64,2048]{1,0:T(8,128)(2,1)S(1)} %collective-permute-done.6.refs_1_, ...), custom_call_target="tpu_custom_call" | custom-call | flops 1879048192 | tf_op jit(solution)/shard_map/project/pallas_call | solution.py:430
  30.7 1.9 %collective-permute-start.12 = (bf16[128,768]{1,0:T(8,128)(2,1)S(1)}, bf16[128,768]{1,0:T(8,128)(2,1)S(1)}, u32[]{:S(2)}, u32[]{:S(2)}) collective-permute-start(bf16[128,768]{1,0:T(8,128)(2,1)S(1)} %get-tuple-element.51), channel_id=1, source_target_pairs={{0,2},{1,3},{2,0},{3,1},{4,6},{5,7},{6,4},{7,5},{8,10},{9,11},{10,... | collective-permute-start | bytes 589832 | tf_op jit(solution)/shard_map/ppermute | solution.py:44
  32.6 1.5 %collective-permute-start.9 = (bf16[128,1024]{1,0:T(8,128)(2,1)S(1)}, bf16[128,1024]{1,0:T(8,128)(2,1)S(1)}, u32[]{:S(2)}, u32[]{:S(2)}) collective-permute-start(bf16[128,1024]{1,0:T(8,128)(2,1)S(1)} %get-tuple-element.49), channel_id=1, source_target_pairs={{0,1},{1,0},{2,3},{3,2},{4,5},{5,4},{6,7},{7,6},{8,9},{9,8},{10,11... | collective-permute-start | bytes 786440 | tf_op jit(solution)/shard_map/ppermute | solution.py:44
  34.1 2.1 %project.3 = (bf16[128,1024]{1,0:T(8,128)(2,1)S(1)}, bf16[128,1024]{1,0:T(8,128)(2,1)S(1)}, bf16[128,768]{1,0:T(8,128)(2,1)S(1)}, bf16[128,768]{1,0:T(8,128)(2,1)S(1)}) custom-call(bf16[64,2048]{1,0:T(8,128)(2,1)S(1)} %far_keys.3.refs_0_, bf16[64,2048]{1,0:T(8,128)(2,1)S(1)} %collective-permute-done.15.refs_1_, ...), custom_call_target="tpu_custom_call" | custom-call | flops 1879048192 | tf_op jit(solution)/shard_map/project/pallas_call | solution.py:430
  37.0 1.1 %collective-permute-done.12 = bf16[128,768]{1,0:T(8,128)(2,1)S(1)} collective-permute-done((bf16[128,768]{1,0:T(8,128)(2,1)S(1)}, bf16[128,768]{1,0:T(8,128)(2,1)S(1)}, u32[]{:S(2)}, u32[]{:S(2)}) %collective-permute-start.12) | collective-permute-done | bytes 196640 | tf_op jit(solution)/shard_map/ppermute | solution.py:44
  38.2 2.8 %collective-permute-start.13 = (bf16[64,768]{1,0:T(8,128)(2,1)S(1)}, bf16[64,768]{1,0:T(8,128)(2,1)S(1)}, u32[]{:S(2)}, u32[]{:S(2)}) collective-permute-start(bf16[64,768]{1,0:T(8,128)(2,1)S(1)} %get-tuple-element.66), channel_id=1, source_target_pairs={{0,4},{1,5},{2,6},{3,7},{4,0},{5,1},{6,2},{7,3},{8,12},{9,13},{10,... | collective-permute-start | bytes 294920 | tf_op jit(solution)/shard_map/ppermute | solution.py:44
  41.0 4.4 %collective-permute-done.21 = bf16[128,768]{1,0:T(8,128)(2,1)S(1)} collective-permute-done((bf16[128,768]{1,0:T(8,128)(2,1)S(1)}, bf16[128,768]{1,0:T(8,128)(2,1)S(1)}, u32[]{:S(2)}, u32[]{:S(2)}) %collective-permute-start.21) | collective-permute-done | bytes 196640 | tf_op jit(solution)/shard_map/ppermute | solution.py:44
  45.4 1.6 %collective-permute-start.22 = (bf16[64,768]{1,0:T(8,128)(2,1)S(1)}, bf16[64,768]{1,0:T(8,128)(2,1)S(1)}, u32[]{:S(2)}, u32[]{:S(2)}) collective-permute-start(bf16[64,768]{1,0:T(8,128)(2,1)S(1)} %get-tuple-element.64), channel_id=1, source_target_pairs={{0,4},{1,5},{2,6},{3,7},{4,0},{5,1},{6,2},{7,3},{8,12},{9,13},{10,... | collective-permute-start | bytes 294920 | tf_op jit(solution)/shard_map/ppermute | solution.py:44
  47.8 1.5 %collective-permute-start.19 = (bf16[64,1024]{1,0:T(8,128)(2,1)S(1)}, bf16[64,1024]{1,0:T(8,128)(2,1)S(1)}, u32[]{:S(2)}, u32[]{:S(2)}) collective-permute-start(bf16[64,1024]{1,0:T(8,128)(2,1)S(1)} %get-tuple-element.60), channel_id=1, source_target_pairs={{0,2},{1,3},{2,0},{3,1},{4,6},{5,7},{6,4},{7,5},{8,10},{9,11},{10,... | collective-permute-start | bytes 393224 | tf_op jit(solution)/shard_map/ppermute | solution.py:44
  49.4 1.6 %collective-permute-start.14 = (bf16[32,768]{1,0:T(8,128)(2,1)S(1)}, bf16[32,768]{1,0:T(8,128)(2,1)S(1)}, u32[]{:S(2)}, u32[]{:S(2)}) collective-permute-start(bf16[32,768]{1,0:T(8,128)(2,1)S(1)} %get-tuple-element.73), channel_id=1, source_target_pairs={{0,1},{1,0},{2,3},{3,2},{4,5},{5,4},{6,7},{7,6},{8,9},{9,8},{10,11... | collective-permute-start | bytes 147464 | tf_op jit(solution)/shard_map/ppermute | solution.py:44
  51.0 3.2 %collective-permute-done.10 = bf16[64,1024]{1,0:T(8,128)(2,1)S(1)} collective-permute-done((bf16[64,1024]{1,0:T(8,128)(2,1)S(1)}, bf16[64,1024]{1,0:T(8,128)(2,1)S(1)}, u32[]{:S(2)}, u32[]{:S(2)}) %collective-permute-start.10) | collective-permute-done | bytes 131104 | tf_op jit(solution)/shard_map/ppermute | solution.py:44
  55.6 1.7 %collective-permute-start.20 = (bf16[32,1024]{1,0:T(8,128)(2,1)S(1)}, bf16[32,1024]{1,0:T(8,128)(2,1)S(1)}, u32[]{:S(2)}, u32[]{:S(2)}) collective-permute-start(bf16[32,1024]{1,0:T(8,128)(2,1)S(1)} %get-tuple-element.67), channel_id=1, source_target_pairs={{0,4},{1,5},{2,6},{3,7},{4,0},{5,1},{6,2},{7,3},{8,12},{9,13},{10,... | collective-permute-start | bytes 196616 | tf_op jit(solution)/shard_map/ppermute | solution.py:44
  57.4 1.6 %collective-permute-start.23 = (bf16[32,768]{1,0:T(8,128)(2,1)S(1)}, bf16[32,768]{1,0:T(8,128)(2,1)S(1)}, u32[]{:S(2)}, u32[]{:S(2)}) collective-permute-start(bf16[32,768]{1,0:T(8,128)(2,1)S(1)} %get-tuple-element.71), channel_id=1, source_target_pairs={{0,1},{1,0},{2,3},{3,2},{4,5},{5,4},{6,7},{7,6},{8,9},{9,8},{10,11... | collective-permute-start | bytes 147464 | tf_op jit(solution)/shard_map/ppermute | solution.py:44
  58.9 2.6 %collective-permute-done.23.refs_7_ = bf16[32,768]{1,0:T(8,128)(2,1)S(1)} collective-permute-done((bf16[32,768]{1,0:T(8,128)(2,1)S(1)}, bf16[32,768]{1,0:T(8,128)(2,1)S(1)}, u32[]{:S(2)}, u32[]{:S(2)}) %collective-permute-start.23) | collective-permute-done | bytes 49184 | tf_op jit(solution)/shard_map/ppermute | solution.py:44
  (52 shorter events, 6.9 us)
Async XLA Ops:
  0.0 6.8 %collective-permute-start.2 = (bf16[576,128]{1,0:T(8,128)(2,1)}, bf16[576,128]{1,0:T(8,128)(2,1)S(1)}, u32[]{:S(2)}, u32[]{:S(2)}) collective-permute-start(bf16[576,128]{1,0:T(8,128)(2,1)} %bitcast.4), channel_id=1, source_target_pairs={{0,8},{8,0},{16,24},{24,16},{1,9},{9,1},{17,25},{25,17},{2,10},{10... | collective-permute-start | bytes 442376 | tf_op jit(solution)/shard_map/ppermute | solution.py:44
  0.5 6.3 %collective-permute-start.3 = (bf16[576,128]{1,0:T(8,128)(2,1)}, bf16[576,128]{1,0:T(8,128)(2,1)S(1)}, u32[]{:S(2)}, u32[]{:S(2)}) collective-permute-start(bf16[576,128]{1,0:T(8,128)(2,1)} %bitcast.7), channel_id=1, source_target_pairs={{0,8},{8,0},{16,24},{24,16},{1,9},{9,1},{17,25},{25,17},{2,10},{10... | collective-permute-start | bytes 442376 | tf_op jit(solution)/shard_map/ppermute | solution.py:44
  0.5 9.3 %collective-permute-start = (bf16[576,128]{1,0:T(8,128)(2,1)}, bf16[576,128]{1,0:T(8,128)(2,1)S(1)}, u32[]{:S(2)}, u32[]{:S(2)}) collective-permute-start(bf16[576,128]{1,0:T(8,128)(2,1)} %bitcast.5), channel_id=1, source_target_pairs={{0,16},{8,24},{16,0},{24,8},{1,17},{9,25},{17,1},{25,9},{2,18},{10... | collective-permute-start | bytes 442376 | tf_op jit(solution)/shard_map/ppermute | solution.py:44
  3.5 7.4 %collective-permute-start.1 = (bf16[576,128]{1,0:T(8,128)(2,1)}, bf16[576,128]{1,0:T(8,128)(2,1)S(1)}, u32[]{:S(2)}, u32[]{:S(2)}) collective-permute-start(bf16[576,128]{1,0:T(8,128)(2,1)} %bitcast.8), channel_id=1, source_target_pairs={{0,16},{8,24},{16,0},{24,8},{1,17},{9,25},{17,1},{25,9},{2,18},{10... | collective-permute-start | bytes 442376 | tf_op jit(solution)/shard_map/ppermute | solution.py:44
  10.8 1.7 %collective-permute-start.4 = (bf16[576,128]{1,0:T(8,128)(2,1)S(1)}, bf16[576,128]{1,0:T(8,128)(2,1)S(1)}, u32[]{:S(2)}, u32[]{:S(2)}) collective-permute-start(bf16[576,128]{1,0:T(8,128)(2,1)S(1)} %collective-permute-done.refs_5_), channel_id=1, source_target_pairs={{0,8},{8,0},{16,24},{24,16},{1,9},{9,1},{17,25},{25,17},{2,10},{10... | collective-permute-start | bytes 442376 | tf_op jit(solution)/shard_map/ppermute | solution.py:44
  10.8 1.7 %collective-permute-start.5 = (bf16[576,128]{1,0:T(8,128)(2,1)S(1)}, bf16[576,128]{1,0:T(8,128)(2,1)S(1)}, u32[]{:S(2)}, u32[]{:S(2)}) collective-permute-start(bf16[576,128]{1,0:T(8,128)(2,1)S(1)} %collective-permute-done.1.refs_6_), channel_id=1, source_target_pairs={{0,8},{8,0},{16,24},{24,16},{1,9},{9,1},{17,25},{25,17},{2,10},{10... | collective-permute-start | bytes 442376 | tf_op jit(solution)/shard_map/ppermute | solution.py:44
  14.5 9.2 %collective-permute-start.7 = (bf16[64,2048]{1,0:T(8,128)(2,1)S(1)}, bf16[64,2048]{1,0:T(8,128)(2,1)S(1)}, u32[]{:S(2)}, u32[]{:S(2)}) collective-permute-start(bf16[64,2048]{1,0:T(8,128)(2,1)S(1)} %far_keys.2.refs_0_), channel_id=1, source_target_pairs={{0,16},{8,24},{16,0},{24,8},{1,17},{9,25},{17,1},{25,9},{2,18},{10... | collective-permute-start | bytes 786440 | tf_op jit(solution)/shard_map/ppermute | solution.py:44
  19.4 9.1 %collective-permute-start.16 = (bf16[64,2048]{1,0:T(8,128)(2,1)S(1)}, bf16[64,2048]{1,0:T(8,128)(2,1)S(1)}, u32[]{:S(2)}, u32[]{:S(2)}) collective-permute-start(bf16[64,2048]{1,0:T(8,128)(2,1)S(1)} %far_keys.3.refs_0_), channel_id=1, source_target_pairs={{0,16},{8,24},{16,0},{24,8},{1,17},{9,25},{17,1},{25,9},{2,18},{10... | collective-permute-start | bytes 786440 | tf_op jit(solution)/shard_map/ppermute | solution.py:44
  19.7 8.8 %collective-permute-start.6 = (bf16[64,2048]{1,0:T(8,128)(2,1)S(1)}, bf16[64,2048]{1,0:T(8,128)(2,1)S(1)}, u32[]{:S(2)}, u32[]{:S(2)}) collective-permute-start(bf16[64,2048]{1,0:T(8,128)(2,1)S(1)} %far_keys.2.refs_0_), channel_id=1, source_target_pairs={{0,8},{8,0},{16,24},{24,16},{1,9},{9,1},{17,25},{25,17},{2,10},{10... | collective-permute-start | bytes 786440 | tf_op jit(solution)/shard_map/ppermute | solution.py:44
  23.7 4.8 %collective-permute-start.8 = (bf16[64,2048]{1,0:T(8,128)(2,1)S(1)}, bf16[64,2048]{1,0:T(8,128)(2,1)S(1)}, u32[]{:S(2)}, u32[]{:S(2)}) collective-permute-start(bf16[64,2048]{1,0:T(8,128)(2,1)S(1)} %collective-permute-done.7.refs_2_), channel_id=1, source_target_pairs={{0,8},{8,0},{16,24},{24,16},{1,9},{9,1},{17,25},{25,17},{2,10},{10... | collective-permute-start | bytes 786440 | tf_op jit(solution)/shard_map/ppermute | solution.py:44
  23.7 10.4 %collective-permute-start.15 = (bf16[64,2048]{1,0:T(8,128)(2,1)S(1)}, bf16[64,2048]{1,0:T(8,128)(2,1)S(1)}, u32[]{:S(2)}, u32[]{:S(2)}) collective-permute-start(bf16[64,2048]{1,0:T(8,128)(2,1)S(1)} %far_keys.3.refs_0_), channel_id=1, source_target_pairs={{0,8},{8,0},{16,24},{24,16},{1,9},{9,1},{17,25},{25,17},{2,10},{10... | collective-permute-start | bytes 786440 | tf_op jit(solution)/shard_map/ppermute | solution.py:44
  28.5 5.6 %collective-permute-start.17 = (bf16[64,2048]{1,0:T(8,128)(2,1)S(1)}, bf16[64,2048]{1,0:T(8,128)(2,1)S(1)}, u32[]{:S(2)}, u32[]{:S(2)}) collective-permute-start(bf16[64,2048]{1,0:T(8,128)(2,1)S(1)} %collective-permute-done.16.refs_2_), channel_id=1, source_target_pairs={{0,8},{8,0},{16,24},{24,16},{1,9},{9,1},{17,25},{25,17},{2,10},{10... | collective-permute-start | bytes 786440 | tf_op jit(solution)/shard_map/ppermute | solution.py:44
  30.7 7.5 %collective-permute-start.12 = (bf16[128,768]{1,0:T(8,128)(2,1)S(1)}, bf16[128,768]{1,0:T(8,128)(2,1)S(1)}, u32[]{:S(2)}, u32[]{:S(2)}) collective-permute-start(bf16[128,768]{1,0:T(8,128)(2,1)S(1)} %get-tuple-element.51), channel_id=1, source_target_pairs={{0,2},{1,3},{2,0},{3,1},{4,6},{5,7},{6,4},{7,5},{8,10},{9,11},{10,... | collective-permute-start | bytes 589832 | tf_op jit(solution)/shard_map/ppermute | solution.py:44
  32.6 14.4 %collective-permute-start.9 = (bf16[128,1024]{1,0:T(8,128)(2,1)S(1)}, bf16[128,1024]{1,0:T(8,128)(2,1)S(1)}, u32[]{:S(2)}, u32[]{:S(2)}) collective-permute-start(bf16[128,1024]{1,0:T(8,128)(2,1)S(1)} %get-tuple-element.49), channel_id=1, source_target_pairs={{0,1},{1,0},{2,3},{3,2},{4,5},{5,4},{6,7},{7,6},{8,9},{9,8},{10,11... | collective-permute-start | bytes 786440 | tf_op jit(solution)/shard_map/ppermute | solution.py:44
  36.2 11.5 %collective-permute-start.18 = (bf16[128,1024]{1,0:T(8,128)(2,1)S(1)}, bf16[128,1024]{1,0:T(8,128)(2,1)S(1)}, u32[]{:S(2)}, u32[]{:S(2)}) collective-permute-start(bf16[128,1024]{1,0:T(8,128)(2,1)S(1)} %get-tuple-element.56), channel_id=1, source_target_pairs={{0,1},{1,0},{2,3},{3,2},{4,5},{5,4},{6,7},{7,6},{8,9},{9,8},{10,11... | collective-permute-start | bytes 786440 | tf_op jit(solution)/shard_map/ppermute | solution.py:44
  36.8 8.6 %collective-permute-start.21 = (bf16[128,768]{1,0:T(8,128)(2,1)S(1)}, bf16[128,768]{1,0:T(8,128)(2,1)S(1)}, u32[]{:S(2)}, u32[]{:S(2)}) collective-permute-start(bf16[128,768]{1,0:T(8,128)(2,1)S(1)} %get-tuple-element.58), channel_id=1, source_target_pairs={{0,2},{1,3},{2,0},{3,1},{4,6},{5,7},{6,4},{7,5},{8,10},{9,11},{10,... | collective-permute-start | bytes 589832 | tf_op jit(solution)/shard_map/ppermute | solution.py:44
  38.2 11.1 %collective-permute-start.13 = (bf16[64,768]{1,0:T(8,128)(2,1)S(1)}, bf16[64,768]{1,0:T(8,128)(2,1)S(1)}, u32[]{:S(2)}, u32[]{:S(2)}) collective-permute-start(bf16[64,768]{1,0:T(8,128)(2,1)S(1)} %get-tuple-element.66), channel_id=1, source_target_pairs={{0,4},{1,5},{2,6},{3,7},{4,0},{5,1},{6,2},{7,3},{8,12},{9,13},{10,... | collective-permute-start | bytes 294920 | tf_op jit(solution)/shard_map/ppermute | solution.py:44
  45.4 11.9 %collective-permute-start.22 = (bf16[64,768]{1,0:T(8,128)(2,1)S(1)}, bf16[64,768]{1,0:T(8,128)(2,1)S(1)}, u32[]{:S(2)}, u32[]{:S(2)}) collective-permute-start(bf16[64,768]{1,0:T(8,128)(2,1)S(1)} %get-tuple-element.64), channel_id=1, source_target_pairs={{0,4},{1,5},{2,6},{3,7},{4,0},{5,1},{6,2},{7,3},{8,12},{9,13},{10,... | collective-permute-start | bytes 294920 | tf_op jit(solution)/shard_map/ppermute | solution.py:44
  47.1 7.1 %collective-permute-start.10 = (bf16[64,1024]{1,0:T(8,128)(2,1)S(1)}, bf16[64,1024]{1,0:T(8,128)(2,1)S(1)}, u32[]{:S(2)}, u32[]{:S(2)}) collective-permute-start(bf16[64,1024]{1,0:T(8,128)(2,1)S(1)} %get-tuple-element.62), channel_id=1, source_target_pairs={{0,2},{1,3},{2,0},{3,1},{4,6},{5,7},{6,4},{7,5},{8,10},{9,11},{10,... | collective-permute-start | bytes 393224 | tf_op jit(solution)/shard_map/ppermute | solution.py:44
  47.8 7.8 %collective-permute-start.19 = (bf16[64,1024]{1,0:T(8,128)(2,1)S(1)}, bf16[64,1024]{1,0:T(8,128)(2,1)S(1)}, u32[]{:S(2)}, u32[]{:S(2)}) collective-permute-start(bf16[64,1024]{1,0:T(8,128)(2,1)S(1)} %get-tuple-element.60), channel_id=1, source_target_pairs={{0,2},{1,3},{2,0},{3,1},{4,6},{5,7},{6,4},{7,5},{8,10},{9,11},{10,... | collective-permute-start | bytes 393224 | tf_op jit(solution)/shard_map/ppermute | solution.py:44
  49.4 9.6 %collective-permute-start.14 = (bf16[32,768]{1,0:T(8,128)(2,1)S(1)}, bf16[32,768]{1,0:T(8,128)(2,1)S(1)}, u32[]{:S(2)}, u32[]{:S(2)}) collective-permute-start(bf16[32,768]{1,0:T(8,128)(2,1)S(1)} %get-tuple-element.73), channel_id=1, source_target_pairs={{0,1},{1,0},{2,3},{3,2},{4,5},{5,4},{6,7},{7,6},{8,9},{9,8},{10,11... | collective-permute-start | bytes 147464 | tf_op jit(solution)/shard_map/ppermute | solution.py:44
  54.2 7.3 %collective-permute-start.11 = (bf16[32,1024]{1,0:T(8,128)(2,1)S(1)}, bf16[32,1024]{1,0:T(8,128)(2,1)S(1)}, u32[]{:S(2)}, u32[]{:S(2)}) collective-permute-start(bf16[32,1024]{1,0:T(8,128)(2,1)S(1)} %get-tuple-element.69), channel_id=1, source_target_pairs={{0,4},{1,5},{2,6},{3,7},{4,0},{5,1},{6,2},{7,3},{8,12},{9,13},{10,... | collective-permute-start | bytes 196616 | tf_op jit(solution)/shard_map/ppermute | solution.py:44
  55.6 5.9 %collective-permute-start.20 = (bf16[32,1024]{1,0:T(8,128)(2,1)S(1)}, bf16[32,1024]{1,0:T(8,128)(2,1)S(1)}, u32[]{:S(2)}, u32[]{:S(2)}) collective-permute-start(bf16[32,1024]{1,0:T(8,128)(2,1)S(1)} %get-tuple-element.67), channel_id=1, source_target_pairs={{0,4},{1,5},{2,6},{3,7},{4,0},{5,1},{6,2},{7,3},{8,12},{9,13},{10,... | collective-permute-start | bytes 196616 | tf_op jit(solution)/shard_map/ppermute | solution.py:44
  57.4 4.2 %collective-permute-start.23 = (bf16[32,768]{1,0:T(8,128)(2,1)S(1)}, bf16[32,768]{1,0:T(8,128)(2,1)S(1)}, u32[]{:S(2)}, u32[]{:S(2)}) collective-permute-start(bf16[32,768]{1,0:T(8,128)(2,1)S(1)} %get-tuple-element.71), channel_id=1, source_target_pairs={{0,1},{1,0},{2,3},{3,2},{4,5},{5,4},{6,7},{7,6},{8,9},{9,8},{10,11... | collective-permute-start | bytes 147464 | tf_op jit(solution)/shard_map/ppermute | solution.py:44
  (5 other events, 37.0 us)
